TPU v7x, 32 devices: a whole 2x2x4 slice. The times are simulated.
32 devices in a mesh: dp: 16 (over z, y, x), tensor: 2 (over core).
Axes of the slice: x: 2, y: 2, z: 4, core: 2. Of those that a mesh axis runs over, the one named last changes fastest.
Arguments:
- inputs: bfloat16 [32768, 768], P('dp'), may hold values from -6 to 6
- segments: int32 [32, 1024], P('dp'), may hold values from 0 to 7, never falling along the last dimension, each value on 1 to 512 neighbouring positions
- cotangent: bfloat16 [32768, 768], P('dp'), may hold values from -6 to 6
- weight_qkv: float32 [3, 768, 768], P(None, 'dp', 'tensor'), may hold values from -0.21875 to 0.21875
- first_qkv: float32 [3, 768, 768], P(None, 'dp', 'tensor'), may hold values from -64 to 64
- second_qkv: float32 [3, 768, 768], P(None, 'dp', 'tensor'), may hold values from 4.096 to 65.536
- weight_out: float32 [768, 768], P(('tensor', 'dp')), may hold values from -0.625 to 0.625
- first_out: float32 [768, 768], P(('tensor', 'dp')), may hold values from -24 to 24
- second_out: float32 [768, 768], P(('tensor', 'dp')), may hold values from 0.65536 to 10.48576
- weight_gate_up: float32 [2, 768, 3072], P(None, 'dp', 'tensor'), may hold values from -0.21875 to 0.21875
- first_gate_up: float32 [2, 768, 3072], P(None, 'dp', 'tensor'), may hold values from -24 to 24
- second_gate_up: float32 [2, 768, 3072], P(None, 'dp', 'tensor'), may hold values from 0.65536 to 10.48576
- weight_down: float32 [3072, 768], P(('tensor', 'dp')), may hold values from -0.109375 to 0.109375
- first_down: float32 [3072, 768], P(('tensor', 'dp')), may hold values from -56 to 56
- second_down: float32 [3072, 768], P(('tensor', 'dp')), may hold values from 3.2768 to 52.4288
- head_bias: float32 [2, 768], P(None, ('tensor', 'dp')), may hold values from -4 to 4
- first_head_bias: float32 [2, 768], P(None, ('tensor', 'dp')), may hold values from -64 to 64
- second_head_bias: float32 [2, 768], P(None, ('tensor', 'dp')), may hold values from 4.096 to 65.536
- norm_vectors: float32 [6, 768], P(None, 'dp'), may hold values from -1.5 to 1.75, as said below
- first_norm_vectors: float32 [6, 768], P(None, 'dp'), may hold values from -80 to 80
- second_norm_vectors: float32 [6, 768], P(None, 'dp'), may hold values from 8.192 to 131.072
Outputs:
- layer_out: bfloat16 [32768, 768], P('dp')
- input_grad: bfloat16 [32768, 768], P('dp')
- grad_qkv: float32 [3, 768, 768], P(None, 'dp', 'tensor')
- new_second_qkv: float32 [3, 768, 768], P(None, 'dp', 'tensor')
- new_weight_qkv: float32 [3, 768, 768], P(None, 'dp', 'tensor')
- grad_out: float32 [768, 768], P(('tensor', 'dp'))
- new_second_out: float32 [768, 768], P(('tensor', 'dp'))
- new_weight_out: float32 [768, 768], P(('tensor', 'dp'))
- grad_gate_up: float32 [2, 768, 3072], P(None, 'dp', 'tensor')
- new_second_gate_up: float32 [2, 768, 3072], P(None, 'dp', 'tensor')
- new_weight_gate_up: float32 [2, 768, 3072], P(None, 'dp', 'tensor')
- grad_down: float32 [3072, 768], P(('tensor', 'dp'))
- new_second_down: float32 [3072, 768], P(('tensor', 'dp'))
- new_weight_down: float32 [3072, 768], P(('tensor', 'dp'))
- grad_head_bias: float32 [2, 768], P(None, ('tensor', 'dp'))
- new_second_head_bias: float32 [2, 768], P(None, ('tensor', 'dp'))
- new_weight_head_bias: float32 [2, 768], P(None, ('tensor', 'dp'))
- grad_norm_vectors: float32 [6, 768], P(None, 'dp')
- new_second_norm_vectors: float32 [6, 768], P(None, 'dp')
- new_weight_norm_vectors: float32 [6, 768], P(None, 'dp')
Inputs may be any that keep to these rules, and one draw needn't show every extreme that they name: `segments`: each row numbers the documents packed into one sequence from 0 upward, never falling; a document has 1 to 512 tokens. `norm_vectors`: rows 2 and 4 lie in 0.25 to 1.75, the other rows in -1.5 to 1.5.
All inputs are finite; a program needn't handle non-finite values.
Results may differ from a plain program's by a relative error of at most 0.025.
Values may be sent and summed in bfloat16 or wider, within the bound.
A program may use at most 192 MiB of HBM per device.

v0:
```python
import math

import jax
import jax.numpy as jnp
import numpy as np
from jax import lax
from jax.sharding import PartitionSpec as P

HEADS = 12
HEAD_DIM = 64
SEQ = 1024
STEP = 10


norm_epsilon = 1e-12
beta_first = 0.9
beta_second = 0.999
adam_epsilon = 1e-08
decay_rate = 0.1
matrix_rate = 0.05
vector_rate = 0.5


def alibi_slopes(head_total):
    power_two = 2 ** int(math.floor(math.log2(head_total)))
    leading = [2.0 ** (-8.0 * (h + 1) / power_two) for h in range(power_two)]
    trailing = [
        2.0 ** (-8.0 * (2 * h + 1) / (2 * power_two)) for h in range(head_total - power_two)
    ]
    return np.array(leading + trailing, dtype=np.float32)


def layer_norm(values, gain, shift):
    centred = values - jnp.mean(values, axis=-1, keepdims=True)
    variance = jnp.mean(centred * centred, axis=-1, keepdims=True)
    return centred * lax.rsqrt(variance + norm_epsilon) * gain + shift


def geglu(gate_up):
    return jax.nn.gelu(gate_up[0], approximate=False) * gate_up[1]


def block_scores(q_rows, k_seq, seg_rows, seg_seq, row_start, slopes):
    block_rows = q_rows.shape[0]
    raw = jnp.einsum("qhd,khd->hqk", q_rows, k_seq, preferred_element_type=jnp.float32)
    row_pos = row_start + jnp.arange(block_rows, dtype=jnp.int32)
    key_pos = jnp.arange(SEQ, dtype=jnp.int32)
    distance = jnp.abs(row_pos[:, None] - key_pos[None, :]).astype(jnp.float32)
    scores = raw * HEAD_DIM ** (-0.5) - slopes[:, None, None] * distance[None]
    allowed = seg_rows[:, None] == seg_seq[None, :]
    return (jnp.where(allowed[None], scores, -1000000000.0), allowed)


def attend_forward(query, keys, values_in, segments, slopes):
    block_rows = min(SEQ, 512)
    block_count = SEQ // block_rows
    head_count = query.shape[2]

    def one_sequence(packed):
        q_seq, k_seq, v_seq, seg_seq = packed

        def one_block(row_start):
            q_rows = lax.dynamic_slice_in_dim(q_seq, row_start, block_rows, 0)
            seg_rows = lax.dynamic_slice_in_dim(seg_seq, row_start, block_rows, 0)
            masked, allowed = block_scores(q_rows, k_seq, seg_rows, seg_seq, row_start, slopes)
            row_max = jnp.max(masked, axis=-1, keepdims=True)
            exp_scores = jnp.exp(masked - row_max)
            row_total = jnp.sum(exp_scores, axis=-1, keepdims=True)
            weights_low = (exp_scores / row_total).astype(jnp.bfloat16)
            context = jnp.einsum(
                "hqk,khd->qhd", weights_low, v_seq, preferred_element_type=jnp.float32
            )
            return (context.astype(jnp.bfloat16), (row_max + jnp.log(row_total))[..., 0])

        starts = jnp.arange(block_count, dtype=jnp.int32) * block_rows
        context, log_total = lax.map(one_block, starts)
        return (context.reshape(SEQ, head_count, HEAD_DIM), log_total)

    return lax.map(one_sequence, (query, keys, values_in, segments))


def attend_backward(query, keys, values_in, segments, d_context, log_total, slopes):
    block_rows = min(SEQ, 512)
    block_count = SEQ // block_rows
    head_count = query.shape[2]
    score_scale = HEAD_DIM ** (-0.5)

    def one_sequence(packed):
        q_seq, k_seq, v_seq, seg_seq, dctx_seq, total_seq = packed
        q_blocks = q_seq.reshape(block_count, block_rows, head_count, HEAD_DIM)
        dctx_blocks = dctx_seq.reshape(block_count, block_rows, head_count, HEAD_DIM)

        def one_block(carry, items):
            d_keys, d_values = carry
            q_rows, dctx_rows, total_rows, block_index = items
            row_start = block_index * block_rows
            seg_rows = lax.dynamic_slice_in_dim(seg_seq, row_start, block_rows, 0)
            masked, allowed = block_scores(q_rows, k_seq, seg_rows, seg_seq, row_start, slopes)
            probs = jnp.where(allowed[None], jnp.exp(masked - total_rows[..., None]), 0.0)
            d_values = d_values + jnp.einsum(
                "hqk,qhd->khd",
                probs.astype(jnp.bfloat16),
                dctx_rows,
                preferred_element_type=jnp.float32,
            )
            d_probs = jnp.einsum(
                "qhd,khd->hqk", dctx_rows, v_seq, preferred_element_type=jnp.float32
            )
            delta = jnp.sum(probs * d_probs, axis=-1, keepdims=True)
            d_scores = (probs * (d_probs - delta)).astype(jnp.bfloat16)
            d_query = (
                jnp.einsum("hqk,khd->qhd", d_scores, k_seq, preferred_element_type=jnp.float32)
                * score_scale
            )
            d_keys = (
                d_keys
                + jnp.einsum("hqk,qhd->khd", d_scores, q_rows, preferred_element_type=jnp.float32)
                * score_scale
            )
            return ((d_keys, d_values), d_query)

        zeros_seq = jnp.zeros((SEQ, head_count, HEAD_DIM), jnp.float32)
        block_ids = jnp.arange(block_count, dtype=jnp.int32)
        (d_keys, d_values), d_query = lax.scan(
            one_block, (zeros_seq, zeros_seq), (q_blocks, dctx_blocks, total_seq, block_ids)
        )
        return (d_query.reshape(SEQ, head_count, HEAD_DIM), d_keys, d_values)

    return lax.map(one_sequence, (query, keys, values_in, segments, d_context, log_total))


def adam_update(weight_old, first_old, second_old, gradient, step_rate):
    first_new = beta_first * first_old + (1.0 - beta_first) * gradient
    second_new = beta_second * second_old + (1.0 - beta_second) * gradient * gradient
    first_hat = first_new / (1.0 - beta_first**STEP)
    second_hat = second_new / (1.0 - beta_second**STEP)
    weight_new = weight_old - step_rate * (
        first_hat / (jnp.sqrt(second_hat) + adam_epsilon) + decay_rate * weight_old
    )
    return (second_new, weight_new)


def shards(
    inputs,
    segments,
    cotangent,
    weight_qkv,
    first_qkv,
    second_qkv,
    weight_out,
    first_out,
    second_out,
    weight_gate_up,
    first_gate_up,
    second_gate_up,
    weight_down,
    first_down,
    second_down,
    head_bias,
    first_head_bias,
    second_head_bias,
    norm_vectors,
    first_norm_vectors,
    second_norm_vectors,
):
    head_count = HEADS // lax.axis_size("tensor")
    all_slopes = jnp.asarray(alibi_slopes(HEADS))
    slopes = lax.dynamic_slice_in_dim(all_slopes, lax.axis_index("tensor") * head_count, head_count)
    proj_qkv, proj_out, proj_gate_up, proj_down, bias_heads, vectors = (
        lax.all_gather(weight_qkv.astype(jnp.bfloat16), "dp", axis=1, tiled=True),
        lax.all_gather(weight_out.astype(jnp.bfloat16), "dp", axis=0, tiled=True),
        lax.all_gather(weight_gate_up.astype(jnp.bfloat16), "dp", axis=1, tiled=True),
        lax.all_gather(weight_down.astype(jnp.bfloat16), "dp", axis=0, tiled=True),
        lax.all_gather(head_bias.astype(jnp.bfloat16), "dp", axis=1, tiled=True),
        lax.all_gather(norm_vectors.astype(jnp.bfloat16), "dp", axis=1, tiled=True),
    )
    bias_heads = bias_heads.astype(jnp.float32)
    vectors = vectors.astype(jnp.float32)
    token_rows = inputs.shape[0]
    seq_count = segments.shape[0]
    group_width = proj_out.shape[0]
    qkv_sum = jnp.einsum("td,cdw->ctw", inputs, proj_qkv, preferred_element_type=jnp.float32)
    qkv_bias = jnp.stack([bias_heads[0], jnp.zeros_like(bias_heads[0]), bias_heads[1]])
    qkv_low = (qkv_sum + qkv_bias[:, None, :]).astype(jnp.bfloat16)
    shaped = qkv_low.reshape(3, seq_count, SEQ, head_count, HEAD_DIM)
    context, log_total = attend_forward(shaped[0], shaped[1], shaped[2], segments, slopes)
    context_low = context.reshape(token_rows, group_width)
    attn_part = jnp.dot(context_low, proj_out, preferred_element_type=jnp.float32)
    attention_out = (
        lax.psum(attn_part.astype(jnp.bfloat16), "tensor").astype(jnp.float32) + vectors[0]
    )
    normed, norm_back_one = jax.vjp(
        layer_norm, inputs.astype(jnp.float32) + attention_out, vectors[2], vectors[3]
    )
    normed_low = normed.astype(jnp.bfloat16)
    gate_up = jnp.einsum(
        "td,cdf->ctf", normed_low, proj_gate_up, preferred_element_type=jnp.float32
    )
    hidden, geglu_back = jax.vjp(geglu, gate_up)
    hidden_low = hidden.astype(jnp.bfloat16)
    ffn_part = jnp.dot(hidden_low, proj_down, preferred_element_type=jnp.float32)
    ffn_out = lax.psum(ffn_part.astype(jnp.bfloat16), "tensor").astype(jnp.float32) + vectors[1]
    result, norm_back_two = jax.vjp(layer_norm, normed + ffn_out, vectors[4], vectors[5])
    layer_out = result.astype(jnp.bfloat16)
    d_second, d_gain_two, d_shift_two = norm_back_two(cotangent.astype(jnp.float32))
    d_ffn_low = d_second.astype(jnp.bfloat16)
    grad_down = jnp.einsum("tf,td->fd", hidden_low, d_ffn_low, preferred_element_type=jnp.float32)
    d_hidden = jnp.einsum("td,fd->tf", d_ffn_low, proj_down, preferred_element_type=jnp.float32)
    (d_gate_up,) = geglu_back(d_hidden)
    d_gate_up_low = d_gate_up.astype(jnp.bfloat16)
    grad_gate_up = jnp.einsum(
        "td,ctf->cdf", normed_low, d_gate_up_low, preferred_element_type=jnp.float32
    )
    back_part = jnp.einsum(
        "ctf,cdf->td", d_gate_up_low, proj_gate_up, preferred_element_type=jnp.float32
    )
    d_normed = d_second + lax.psum(back_part.astype(jnp.bfloat16), "tensor").astype(jnp.float32)
    d_first, d_gain_one, d_shift_one = norm_back_one(d_normed)
    d_attn_low = d_first.astype(jnp.bfloat16)
    grad_out = jnp.einsum("tw,td->wd", context_low, d_attn_low, preferred_element_type=jnp.float32)
    d_context = jnp.einsum(
        "td,wd->tw", d_attn_low, proj_out, preferred_element_type=jnp.float32
    ).astype(jnp.bfloat16)
    d_query, d_keys, d_values = attend_backward(
        shaped[0],
        shaped[1],
        shaped[2],
        segments,
        d_context.reshape(seq_count, SEQ, head_count, HEAD_DIM),
        log_total,
        slopes,
    )
    d_qkv_low = (
        jnp.stack([d_query, d_keys, d_values])
        .reshape(3, token_rows, group_width)
        .astype(jnp.bfloat16)
    )
    grad_qkv = jnp.einsum("td,ctw->cdw", inputs, d_qkv_low, preferred_element_type=jnp.float32)
    grad_heads = jnp.stack(
        [
            jnp.sum(d_qkv_low[0], axis=0, dtype=jnp.float32),
            jnp.sum(d_qkv_low[2], axis=0, dtype=jnp.float32),
        ]
    )
    input_part = jnp.einsum("ctw,cdw->td", d_qkv_low, proj_qkv, preferred_element_type=jnp.float32)
    input_grad = (
        d_first + lax.psum(input_part.astype(jnp.bfloat16), "tensor").astype(jnp.float32)
    ).astype(jnp.bfloat16)
    grad_vectors = jnp.stack(
        [
            jnp.sum(d_first, axis=0),
            jnp.sum(d_second, axis=0),
            d_gain_one,
            d_shift_one,
            d_gain_two,
            d_shift_two,
        ]
    )
    grad_qkv, grad_out, grad_gate_up, grad_down, grad_heads, grad_vectors = (
        lax.psum_scatter(grad_qkv, "dp", scatter_dimension=1, tiled=True),
        lax.psum_scatter(grad_out, "dp", scatter_dimension=0, tiled=True),
        lax.psum_scatter(grad_gate_up, "dp", scatter_dimension=1, tiled=True),
        lax.psum_scatter(grad_down, "dp", scatter_dimension=0, tiled=True),
        lax.psum_scatter(grad_heads, "dp", scatter_dimension=1, tiled=True),
        lax.psum_scatter(grad_vectors, "dp", scatter_dimension=1, tiled=True),
    )
    second_qkv_new, weight_qkv_new = adam_update(
        weight_qkv, first_qkv, second_qkv, grad_qkv, matrix_rate
    )
    second_out_new, weight_out_new = adam_update(
        weight_out, first_out, second_out, grad_out, matrix_rate
    )
    second_gu_new, weight_gu_new = adam_update(
        weight_gate_up, first_gate_up, second_gate_up, grad_gate_up, matrix_rate
    )
    second_down_new, weight_down_new = adam_update(
        weight_down, first_down, second_down, grad_down, matrix_rate
    )
    second_heads_new, weight_heads_new = adam_update(
        head_bias, first_head_bias, second_head_bias, grad_heads, vector_rate
    )
    second_vectors_new, weight_vectors_new = adam_update(
        norm_vectors, first_norm_vectors, second_norm_vectors, grad_vectors, vector_rate
    )
    return (
        layer_out,
        input_grad,
        grad_qkv,
        second_qkv_new,
        weight_qkv_new,
        grad_out,
        second_out_new,
        weight_out_new,
        grad_gate_up,
        second_gu_new,
        weight_gu_new,
        grad_down,
        second_down_new,
        weight_down_new,
        grad_heads,
        second_heads_new,
        weight_heads_new,
        grad_vectors,
        second_vectors_new,
        weight_vectors_new,
    )


def solution(mesh):
    in_specs = (
        P("dp", None),
        P("dp", None),
        P("dp", None),
        P(None, "dp", "tensor"),
        P(None, "dp", "tensor"),
        P(None, "dp", "tensor"),
        P(("tensor", "dp"), None),
        P(("tensor", "dp"), None),
        P(("tensor", "dp"), None),
        P(None, "dp", "tensor"),
        P(None, "dp", "tensor"),
        P(None, "dp", "tensor"),
        P(("tensor", "dp"), None),
        P(("tensor", "dp"), None),
        P(("tensor", "dp"), None),
        P(None, ("tensor", "dp")),
        P(None, ("tensor", "dp")),
        P(None, ("tensor", "dp")),
        P(None, "dp"),
        P(None, "dp"),
        P(None, "dp"),
    )
    out_specs = (
        P("dp", None),
        P("dp", None),
        P(None, "dp", "tensor"),
        P(None, "dp", "tensor"),
        P(None, "dp", "tensor"),
        P(("tensor", "dp"), None),
        P(("tensor", "dp"), None),
        P(("tensor", "dp"), None),
        P(None, "dp", "tensor"),
        P(None, "dp", "tensor"),
        P(None, "dp", "tensor"),
        P(("tensor", "dp"), None),
        P(("tensor", "dp"), None),
        P(("tensor", "dp"), None),
        P(None, ("tensor", "dp")),
        P(None, ("tensor", "dp")),
        P(None, ("tensor", "dp")),
        P(None, "dp"),
        P(None, "dp"),
        P(None, "dp"),
    )
    return jax.shard_map(shards, mesh=mesh, in_specs=in_specs, out_specs=out_specs, check_vma=False)
```

profile of v0, /device:TPU:0, one launch (start us, length us, event | category | flops | bytes accessed | tf_op | source)
XLA Modules:
  0.0 1555.5 jit_solution(14470191113237648063)
XLA Ops:
  9.6 42.2 %all-gather = bf16[16,24,2]{1,2,0:T(2,128)(2,1)S(1)} all-gather(bf16[1,24,2]{1,2,0:T(2,128)(2,1)S(1)} %convert_bitcast_fusion.1), channel_id=1, replica_groups=mesh['dp'=16,'tensor'=2] {'dp'}, dimensions={0}, use_global_device_ids=true | all-gather | bytes 1632 | tf_op jit(solution)/shard_map/all_gather | solution.py:174
  53.7 42.2 %all_gather.20 = bf16[384,768]{1,0:T(8,128)(2,1)} all-gather(bf16[24,768]{1,0:T(8,128)(2,1)S(1)} %convert_element_type.128), channel_id=1, replica_groups=mesh['dp'=16,'tensor'=2] {'dp'}, dimensions={0}, use_global_device_ids=true | all-gather | bytes 626688 | tf_op jit(solution)/shard_map/all_gather | solution.py:171
  119.8 92.4 %while.54 = (s32[]{:T(128)}, bf16[2,1024,6,64]{3,2,1,0:T(8,128)(2,1)}, f32[2,2,6,512]{3,2,1,0:T(8,128)S(1)}, bf16[2,1024,6,64]{1,3,2,0:T(8,128)(2,1)}, s32[2,102...) while((s32[]{:T(128)}, ...), condition=%wide.region_5.6_spmd, body=%wide.region_0.5_spmd.sunk | while | flops 864220672 | bytes 59977184 | solution.py:79
  124.1 38.7 %while.57 = (s32[]{:T(128)}, bf16[2,512,6,64]{1,3,2,0:T(8,128)(2,1)S(1)}, f32[2,6,512]{2,1,0:T(8,128)S(1)}, s32[2]{0:T(128)S(1)}, s32[1024]{0:T(1024)S(1)}, /*in...) while((s32[]{:T(128)}, ...), condition=%wide.region_4.4_spmd, body=%wide.region_1.3_spmd.sunk | while | flops 864220672 | bytes 50728152 | solution.py:76
  170.4 38.7 %while.57 = (s32[]{:T(128)}, bf16[2,512,6,64]{1,3,2,0:T(8,128)(2,1)S(1)}, f32[2,6,512]{2,1,0:T(8,128)S(1)}, s32[2]{0:T(128)S(1)}, s32[1024]{0:T(1024)S(1)}, /*in...) while((s32[]{:T(128)}, ...), condition=%wide.region_4.4_spmd, body=%wide.region_1.3_spmd.sunk | while | flops 864220672 | bytes 50728152 | solution.py:76
  226.9 37.4 %all-gather.1 = bf16[16,48,6]{1,2,0:T(8,128)(2,1)S(1)} all-gather(bf16[1,48,6]{1,2,0:T(8,128)(2,1)S(1)} %convert_bitcast_fusion), channel_id=1, replica_groups=mesh['dp'=16,'tensor'=2] {'dp'}, dimensions={0}, use_global_device_ids=true | all-gather | bytes 9792 | tf_op jit(solution)/shard_map/all_gather | solution.py:175
  269.5 60.8 %all-gather.8.cloned.1.call-done = bf16[2,768,1536]{2,1,0:T(8,128)(2,1)} async-done(((bf16[2,48,1536]{2,1,0:T(8,128)(2,1)}), bf16[2,768,1536]{2,1,0:T(8,128)(2,1)}) %all-gather.8.cloned.1.call-update) | async-done | bytes 4718608 | tf_op jit(solution)/shard_map/all_gather | solution.py:172
  330.3 18.2 %convolution_bitcast_fusion = f32[2,2048,1536]{2,1,0:T(8,128)} fusion(bf16[2,768,1536]{2,1,0:T(8,128)(2,1)} %all-gather.8.cloned.1.call-done, f32[768]{0:T(1024)S(1)} %get-tuple-element.480, f32[768]{0:T(1024)S(1)} %get-tuple-element.481, f32[2048]{0:T(1024)S(1)} %fusion.69, bf16[2048,768]{1,0:T(8,128)(2,1)} %all-reduce.12.cloned.1.call-done, ...), kind=kOutput, calls=%fused_computation.63 | convolution fusion | flops 9677832192 | bytes 36201472 | tf_op jit(solution)/shard_map/td,cdf->ctf/dot_general | solution.py:196
  348.5 29.9 %multiply_convert_fusion.1 = (bf16[2048,1536]{1,0:T(8,128)(2,1)}, f32[2048,1536]{1,0:T(8,128)}) fusion(f32[2,2048,1536]{2,1,0:T(8,128)} %convolution_bitcast_fusion), kind=kLoop, calls=%fused_computation.80 | loop fusion | flops 207618048 | bytes 44040192 | tf_op jit(solution)/shard_map/convert_element_type | solution.py:200
  378.4 16.5 %all-gather.10.cloned.1.call-done = bf16[1536,768]{1,0:T(8,128)(2,1)} async-done(((bf16[96,768]{1,0:T(8,128)(2,1)}), bf16[1536,768]{1,0:T(8,128)(2,1)}) %all-gather.10.cloned.1.call-update) | async-done | bytes 2359312 | tf_op jit(solution)/shard_map/all_gather | solution.py:173
  404.0 22.1 %all-reduce.14.cloned.1.call-done = bf16[2048,768]{1,0:T(8,128)(2,1)} async-done(((bf16[2048,768]{1,0:T(8,128)(2,1)}), bf16[2048,768]{1,0:T(8,128)(2,1)}) %all-reduce.14.cloned.1.call-update) | async-done | bytes 3145744 | tf_op jit(solution)/shard_map/psum | solution.py:202
  441.3 26.9 %multiply_bitcast_fusion = (f32[1,2048,1536]{2,1,0:T(8,128)}, f32[1,2048,1536]{2,1,0:T(8,128)}) fusion(f32[2048,1536]{1,0:T(8,128)} %get-tuple-element.587, f32[2,2048,1536]{2,1,0:T(8,128)} %convolution_bitcast_fusion, bf16[1536,768]{1,0:T(8,128)(2,1)} %all-gather.10.cloned.1.call-done, f32[2048,768]{1,0:T(8,128)} %get-tuple-element.583, ...), kind=kOutput, calls=%fused_computation.79 | convolution fusion | flops 4885315584 | bytes 71573504 | tf_op jit(solution)/shard_map/td,fd->tf/dot_general | solution.py:208
  468.2 17.2 %bitcast_convert_fusion.1 = bf16[2048,768]{1,0:T(8,128)(2,1)} fusion(bf16[2,768,1536]{2,1,0:T(8,128)(2,1)} %all-gather.8.cloned.1.call-done, f32[1,2048,1536]{2,1,0:T(8,128)} %get-tuple-element.597, f32[1,2048,1536]{2,1,0:T(8,128)} %get-tuple-element.596), kind=kOutput, calls=%fused_computation.106 | convolution fusion | flops 9677832192 | bytes 33030144 | tf_op jit(solution)/shard_map/ctf,cdf->td/dot_general | solution.py:214
  485.6 24.5 %all-reduce.16.cloned.1.call-done = bf16[2048,768]{1,0:T(8,128)(2,1)} async-done(((bf16[2048,768]{1,0:T(8,128)(2,1)}), bf16[2048,768]{1,0:T(8,128)(2,1)}) %all-reduce.16.cloned.1.call-update) | async-done | bytes 3145744 | tf_op jit(solution)/shard_map/psum | solution.py:217
  510.1 9.3 multiply_reduce_fusion.1
  533.6 156.2 %while.56 = (s32[]{:T(128)}, bf16[2,1024,6,64]{3,2,1,0:T(8,128)(2,1)}, bf16[2,1024,6,64]{1,3,2,0:T(8,128)(2,1)}, bf16[2,1024,6,64]{1,3,2,0:T(8,128)(2,1)}, bf16[...) while((s32[]{:T(128)}, ...), condition=%wide.region_21.22_spmd, body=%wide.region_17.21_spmd.sunk | while | flops 2055271936 | bytes 154672448 | solution.py:129
  544.1 59.3 %while.58 = (s32[]{:T(128)}, f32[1024,6,64]{0,2,1:T(8,128)S(1)}, f32[1024,6,64]{0,2,1:T(8,128)S(1)}, bf16[2,512,6,64]{1,3,2,0:T(8,128)(2,1)}, bf16[2,512,6,64]{1...) while((s32[]{:T(128)}, f32[1024,6,64]{0,2,1:T(8,128)S(1)}, ...), condition=%wide.region_20.20_spmd.clone, body=%wide.region_18.19_spmd.clone.sunk | while | flops 2055271936 | bytes 129579936 | solution.py:124
  553.9 9.3 multiply_reduce_fusion.6
  583.6 9.3 multiply_reduce_fusion.6
  621.9 59.3 %while.58 = (s32[]{:T(128)}, f32[1024,6,64]{0,2,1:T(8,128)S(1)}, f32[1024,6,64]{0,2,1:T(8,128)S(1)}, bf16[2,512,6,64]{1,3,2,0:T(8,128)(2,1)}, bf16[2,512,6,64]{1...) while((s32[]{:T(128)}, f32[1024,6,64]{0,2,1:T(8,128)S(1)}, ...), condition=%wide.region_20.20_spmd.clone, body=%wide.region_18.19_spmd.clone.sunk | while | flops 2055271936 | bytes 129579936 | solution.py:124
  631.8 9.3 multiply_reduce_fusion.6
  661.4 9.3 multiply_reduce_fusion.6
  709.1 9.1 bitcast_convert_fusion
  723.8 19.0 %all-reduce.18.cloned.1.call-done = bf16[2048,768]{1,0:T(8,128)(2,1)} async-done(((bf16[2048,768]{1,0:T(8,128)(2,1)}), bf16[2048,768]{1,0:T(8,128)(2,1)}) %all-reduce.18.cloned.1.call-update) | async-done | bytes 3145744 | tf_op jit(solution)/shard_map/psum | solution.py:247
  749.3 10.9 fusion.77
  760.4 19.8 %convolution_bitcast_fusion.1 = f32[2,768,1536]{1,2,0:T(8,128)} fusion(f32[1,2048,1536]{2,1,0:T(8,128)} %get-tuple-element.597, f32[1,2048,1536]{2,1,0:T(8,128)} %get-tuple-element.596, f32[768]{0:T(1024)S(1)} %copy-done.45, f32[768]{0:T(1024)S(1)} %copy-done.38, f32[2048]{0:T(1024)S(1)} %copy-done.32, ...), kind=kOutput, calls=%fused_computation.123 | convolution fusion | flops 9690415104 | bytes 40920064 | tf_op jit(solution)/shard_map/td,ctf->cdf/dot_general | solution.py:211
  780.1 15.0 copy.179
  814.5 42.0 %all-reduce.4 = f32[2,384]{1,0:T(2,128)S(1)} all-reduce(f32[2,384]{1,0:T(2,128)S(1)} %pad_maximum_fusion.4), channel_id=6, replica_groups=mesh['dp'=16,'tensor'=2] {'dp'}, use_global_device_ids=true, to_apply=%region_29.30.clone | all-reduce | flops 768 | bytes 6144
  857.1 15.7 %reduce-scatter.7.cloned.1.call-done = f32[24,768]{1,0:T(8,128)} async-done(((f32[384,768]{1,0:T(8,128)}), f32[24,768]{1,0:T(8,128)}) %reduce-scatter.7.cloned.1.call-update) | async-done | bytes 73744 | tf_op jit(solution)/shard_map/reduce_scatter | solution.py:261
  874.5 124.1 %reduce-scatter.11.cloned.1.call-done = f32[48,6]{1,0:T(8,128)} async-done(((f32[768,6]{1,0:T(8,128)}), f32[48,6]{1,0:T(8,128)}) %reduce-scatter.11.cloned.1.call-update) | async-done | bytes 1168
  1000.1 140.8 %reduce-scatter.9.cloned.1.call-done = f32[96,768]{1,0:T(8,128)} async-done(((f32[1536,768]{1,0:T(8,128)}), f32[96,768]{1,0:T(8,128)}) %reduce-scatter.9.cloned.1.call-update) | async-done | bytes 294928 | tf_op jit(solution)/shard_map/reduce_scatter | solution.py:263
  1143.1 399.1 %all-reduce.20.cloned.1.call-done = (f32[3,768,384]{2,0,1:T(4,128)}, f32[2,768,1536]{2,0,1:T(2,128)}) async-done(((f32[3,768,384]{2,0,1:T(4,128)}, f32[2,768,1536]{2,0,1:T(2,128)}), (f32[3,768,384]{2,0,1:T(4,128)}, f32[2,768,1536]{2,0,1:T(2,128)})) %all-reduce.20.cloned.1.call-update) | async-done | bytes 12976144
  (391 shorter events, 347.8 us)
Async XLA Ops:
  7.2 88.8 %all-gather.6.cloned.1.call-start = ((), (), s32[]{:S(2)}) async-start(), calls=%async_computation.3 | async-start | bytes 1880064 | tf_op jit(solution)/shard_map/all_gather | solution.py:170
  8.9 255.7 %all-reduce.12.cloned.1.call-start = ((), (), s32[]{:S(2)}) async-start(), calls=%async_computation.4 | async-start | bytes 6291456 | tf_op jit(solution)/shard_map/psum | solution.py:190
  219.0 45.5 %copy-start.4 = (bf16[2048,768]{1,0:T(8,128)(2,1)S(1)}, bf16[2048,768]{1,0:T(8,128)(2,1)}, u32[]{:S(2)}) copy-start(bf16[2048,768]{1,0:T(8,128)(2,1)} %param.30) | copy-start | bytes 9437188
  224.2 106.1 %all-gather.8.cloned.1.call-start = ((), (), s32[]{:S(2)}) async-start(), calls=%async_computation.5 | async-start | bytes 5013504 | tf_op jit(solution)/shard_map/all_gather | solution.py:172
  226.1 168.8 %all-gather.10.cloned.1.call-start = ((), (), s32[]{:S(2)}) async-start(), calls=%async_computation.6 | async-start | bytes 2506752 | tf_op jit(solution)/shard_map/all_gather | solution.py:173
  226.8 199.3 %all-reduce.14.cloned.1.call-start = ((), (), s32[]{:S(2)}) async-start(), calls=%async_computation.7 | async-start | bytes 6291456 | tf_op jit(solution)/shard_map/psum | solution.py:202
  264.5 161.6 %copy-start.44 = (f32[768]{0:T(1024)}, f32[768]{0:T(1024)S(1)}, u32[]{:S(2)}) copy-start(f32[768]{0:T(1024)S(1)} %get-tuple-element.480) | copy-start | bytes 9220
  264.5 254.9 %copy-start.29 = (f32[768]{0:T(1024)}, f32[768]{0:T(1024)S(1)}, u32[]{:S(2)}) copy-start(f32[768]{0:T(1024)S(1)} %get-tuple-element.482) | copy-start | bytes 9220
  264.5 254.9 %copy-start.37 = (f32[768]{0:T(1024)}, f32[768]{0:T(1024)S(1)}, u32[]{:S(2)}) copy-start(f32[768]{0:T(1024)S(1)} %get-tuple-element.481) | copy-start | bytes 9220
  267.7 251.7 %copy-start.27 = (f32[2048]{0:T(1024)}, f32[2048]{0:T(1024)S(1)}, u32[]{:S(2)}) copy-start(f32[2048]{0:T(1024)S(1)} %broadcast_multiply_fusion.1) | copy-start | bytes 24580
  269.5 249.9 %copy-start.31 = (f32[2048]{0:T(1024)}, f32[2048]{0:T(1024)S(1)}, u32[]{:S(2)}) copy-start(f32[2048]{0:T(1024)S(1)} %fusion.69) | copy-start | bytes 24580
  403.9 106.1 %all-reduce.16.cloned.1.call-start = ((), (), s32[]{:S(2)}) async-start(), calls=%async_computation.8 | async-start | bytes 6291456 | tf_op jit(solution)/shard_map/psum | solution.py:217
  441.3 78.1 %copy-start.33 = (f32[2048]{0:T(1024)}, f32[2048]{0:T(1024)S(1)}, u32[]{:S(2)}) copy-start(f32[2048]{0:T(1024)S(1)} %negate_multiply_fusion.2) | copy-start | bytes 24580
  485.5 257.3 %all-reduce.18.cloned.1.call-start = ((), (), s32[]{:S(2)}) async-start(), calls=%async_computation.9 | async-start | bytes 6291456 | tf_op jit(solution)/shard_map/psum | solution.py:247
  694.1 13.2 copy-start.11
  718.2 154.6 %reduce-scatter.7.cloned.1.call-start = ((), (), s32[]{:S(2)}) async-start(), calls=%async_computation.10 | async-start | bytes 1253376 | tf_op jit(solution)/shard_map/reduce_scatter | solution.py:261
  723.6 275.0 %reduce-scatter.11.cloned.1.call-start = ((), (), s32[]{:S(2)}) async-start(), calls=%async_computation.12 | async-start | bytes 417792
  723.8 25.5 %copy-start.34 = (f32[2048]{0:T(1024)S(1)}, f32[2048]{0:T(1024)}, u32[]{:S(2)}) copy-start(f32[2048]{0:T(1024)} %copy-done.33) | copy-start | bytes 24580
  749.2 11.1 copy-start.5
  749.3 391.6 %reduce-scatter.9.cloned.1.call-start = ((), (), s32[]{:S(2)}) async-start(), calls=%async_computation.11 | async-start | bytes 5013504 | tf_op jit(solution)/shard_map/reduce_scatter | solution.py:263
  760.3 781.9 %all-reduce.20.cloned.1.call-start = ((), (), s32[]{:S(2)}) async-start(), calls=%async_computation.13 | async-start | bytes 28311552
  809.6 46.9 %copy-start.51 = (f32[2,24]{1,0:T(2,128)S(1)}, f32[2,24]{1,0:T(2,128)}, u32[]{:S(2)}) copy-start(f32[2,24]{1,0:T(2,128)} %param.45) | copy-start | bytes 580
  809.6 46.9 %copy-start.52 = (f32[2,24]{1,0:T(2,128)S(1)}, f32[2,24]{1,0:T(2,128)}, u32[]{:S(2)}) copy-start(f32[2,24]{1,0:T(2,128)} %param.46) | copy-start | bytes 580
  809.6 46.9 %copy-start.53 = (f32[2,24]{1,0:T(2,128)S(1)}, f32[2,24]{1,0:T(2,128)}, u32[]{:S(2)}) copy-start(f32[2,24]{1,0:T(2,128)} %param.47) | copy-start | bytes 580
  809.6 63.2 %copy-start.26 = (f32[24,768]{1,0:T(8,128)S(1)}, f32[24,768]{1,0:T(8,128)}, u32[]{:S(2)}) copy-start(f32[24,768]{1,0:T(8,128)} %param.36) | copy-start | bytes 221188
  809.7 189.8 %copy-start.48 = (f32[6,48]{1,0:T(8,128)S(1)}, f32[6,48]{1,0:T(8,128)}, u32[]{:S(2)}) copy-start(f32[6,48]{1,0:T(8,128)} %param.48) | copy-start | bytes 3460
  809.7 189.8 %copy-start.49 = (f32[6,48]{1,0:T(8,128)S(1)}, f32[6,48]{1,0:T(8,128)}, u32[]{:S(2)}) copy-start(f32[6,48]{1,0:T(8,128)} %param.49) | copy-start | bytes 3460
  809.7 189.8 %copy-start.50 = (f32[6,48]{1,0:T(8,128)S(1)}, f32[6,48]{1,0:T(8,128)}, u32[]{:S(2)}) copy-start(f32[6,48]{1,0:T(8,128)} %param.50) | copy-start | bytes 3460
  809.7 331.2 %copy-start.19 = (f32[96,768]{1,0:T(8,128)S(1)}, f32[96,768]{1,0:T(8,128)}, u32[]{:S(2)}) copy-start(f32[96,768]{1,0:T(8,128)} %param.42) | copy-start | bytes 884740
  814.1 732.2 %copy-start.16 = (f32[2,48,1536]{2,1,0:T(8,128)S(1)}, f32[2,48,1536]{2,1,0:T(8,128)}, u32[]{:S(2)}) copy-start(f32[2,48,1536]{2,1,0:T(8,128)} %param.39) | copy-start | bytes 1769476
  814.1 732.2 %copy-start.21 = (f32[2,48,1536]{2,1,0:T(8,128)S(1)}, f32[2,48,1536]{2,1,0:T(8,128)}, u32[]{:S(2)}) copy-start(f32[2,48,1536]{2,1,0:T(8,128)} %param.40) | copy-start | bytes 1769476
  999.5 549.4 %copy-start.46 = (f32[6,48]{1,0:T(8,128)}, f32[6,48]{1,0:T(8,128)S(1)}, u32[]{:S(2)}) copy-start(f32[6,48]{1,0:T(8,128)S(1)} %copy.192) | copy-start | bytes 3460
  (54 other events, 316.1 us)
Sparse Core Ops, SparseCore 0:
  11.3 64.7 all-gather.5
  224.3 20.6 all-reduce.11
  248.6 81.6 all-gather.7
  333.9 60.9 all-gather.9
  404.0 22.0 all-reduce.13
  485.6 24.3 all-reduce.15
  718.4 24.3 all-reduce.17
  748.1 124.7 reduce-scatter.6
  878.1 120.4 reduce-scatter.10
  1005.0 135.8 reduce-scatter.8
  1147.3 394.7 all-reduce.19
where the time goes:
time: 1560 us
  waiting for transfers between devices  823 us (53%)
  matrix products  268 us (17%)
  blocking collectives  164 us (11%)
  local copies, waits for them, and re-layouts  137 us (9%)
  other arithmetic  136 us (9%)
  between operations  16.2 us (1%)
    unnamed x13, waiting for transfers between devices  523 us
    reduce_scatter x1, waiting for transfers between devices, shards(): lax.psum_scatter(grad_down, 'dp', scatter_dimension=0, tiled=True)  141 us
    all_gather x1, waiting for transfers between devices, shards(): lax.all_gather(weight_gate_up.astype(jnp.bfloat16), 'dp', axis=1, tiled=T...  60.8 us
    dot_general x8, matrix products, block_scores(): jnp.einsum('qhd,khd->hqk', q_rows, k_seq, preferred_element_type=jnp.floa...  60.1 us
    all_gather x1, blocking collectives, shards(): lax.all_gather(weight_out.astype(jnp.bfloat16), 'dp', axis=0, tiled=True)  42.2 us
    all_gather x1, blocking collectives, shards(): lax.all_gather(head_bias.astype(jnp.bfloat16), 'dp', axis=1, tiled=True)  42.2 us
    unnamed x1, blocking collectives  42 us
    all_gather x1, blocking collectives, shards(): lax.all_gather(norm_vectors.astype(jnp.bfloat16), 'dp', axis=1, tiled=True)  37.4 us
  transfers between devices with their start and end apart: 11, of which 9 were waited for; matrix products, arithmetic and copies ran while one was open for 9% of the time, Pallas kernels for 0%

commit v1 on v0

--- a/solution.py
+++ b/solution.py
@@ -4,7 +4,12 @@
 import jax.numpy as jnp
 import numpy as np
 from jax import lax
+from jax.experimental import pallas as pl
+from jax.experimental.pallas import tpu as pltpu
 from jax.sharding import PartitionSpec as P
+
+MESH = pl.DeviceIdType.MESH
+TORUS = (4, 2, 2)
 
 HEADS = 12
 HEAD_DIM = 64
@@ -140,6 +145,290 @@
     return (second_new, weight_new)
 
 
+def place():
+    me = lax.axis_index("dp")
+    return lax.div(me, 4), lax.rem(lax.div(me, 2), 2), lax.rem(me, 2)
+
+def rdma(src, dst, ssem, rsem, dev):
+    return pltpu.make_async_remote_copy(src_ref=src, dst_ref=dst, send_sem=ssem, recv_sem=rsem, device_id={"dp": dev}, device_id_type=MESH)
+
+class Gather:
+    def s0(self): self.start_z()
+    def s1(self): self.wait_z(); self.start_p(0)
+    def s2(self): self.wait_p(0); self.start_p(1)
+    def s3(self): self.wait_p(1)
+
+    def __init__(self, src, dst, first, ssem, rsem, lsem):
+        self.src, self.dst, self.first, self.ssem, self.rsem, self.lsem = src, dst, first, ssem, rsem, lsem
+        self.z, self.y, self.x = place()
+    def zcopy(self, d):
+        z, y, x = self.z, self.y, self.x
+        zt = lax.rem(z + d, 4); zs = lax.rem(z + 4 - d, 4)
+        c = rdma(self.src, self.dst(z, y, x), self.ssem.at[d - 1], self.rsem.at[d - 1], zt * 4 + y * 2 + x)
+        r = rdma(self.src, self.dst(zs, y, x), self.ssem.at[d - 1], self.rsem.at[d - 1], zs * 4 + y * 2 + x)
+        return c, r
+    def start_z(self):
+        pltpu.make_async_copy(self.src, self.dst(self.z, self.y, self.x), self.lsem).start()
+        for d in (1, 3, 2):
+            self.zcopy(d)[0].start()
+    def wait_z(self):
+        pltpu.make_async_copy(self.src, self.dst(self.z, self.y, self.x), self.lsem).wait()
+        for d in (1, 3, 2):
+            c, r = self.zcopy(d); c.wait_send(); r.wait_recv()
+    def plane(self, k):
+        z, y, x = self.z, self.y, self.x
+        al = slice(None)
+        if self.first == 'x':
+            if k == 0:
+                mine, theirs, dev = self.dst(al, y, x), self.dst(al, y, 1 - x), z * 4 + y * 2 + 1 - x
+            else:
+                mine, theirs, dev = self.dst(al, y, al), self.dst(al, 1 - y, al), z * 4 + (1 - y) * 2 + x
+        else:
+            if k == 0:
+                mine, theirs, dev = self.dst(al, y, x), self.dst(al, 1 - y, x), z * 4 + (1 - y) * 2 + x
+            else:
+                mine, theirs, dev = self.dst(al, al, x), self.dst(al, al, 1 - x), z * 4 + y * 2 + 1 - x
+        c = rdma(mine, mine, self.ssem.at[3 + k], self.rsem.at[3 + k], dev)
+        r = rdma(theirs, theirs, self.ssem.at[3 + k], self.rsem.at[3 + k], dev)
+        return c, r
+    def start_p(self, k):
+        self.plane(k)[0].start()
+    def wait_p(self, k):
+        c, r = self.plane(k); c.wait_send(); r.wait_recv()
+
+def enter():
+    z, y, x = place()
+    peers = [lax.rem(z + d, 4) * 4 + y * 2 + x for d in (1, 2, 3)] + [z * 4 + (1 - y) * 2 + x, z * 4 + y * 2 + 1 - x]
+    b = pltpu.get_barrier_semaphore()
+    for p in peers:
+        pl.semaphore_signal(b, inc=1, device_id={"dp": p}, device_id_type=MESH)
+    pl.semaphore_wait(b, 5)
+
+class Scatter:
+    def __init__(self, g, r1, r2, r3, out, first, ssem, rsem):
+        self.g, self.r1, self.r2, self.r3, self.out, self.first, self.ssem, self.rsem = g, r1, r2, r3, out, first, ssem, rsem
+        z, y, x = self.z, self.y, self.x = place()
+        if first == 'y':
+            self.sel = lambda zz, a, b: g(zz, a, b)
+            self.a, self.b = y, x
+            self.d1, self.d2 = z * 4 + (1 - y) * 2 + x, z * 4 + y * 2 + 1 - x
+        else:
+            self.sel = lambda zz, a, b: g(zz, b, a)
+            self.a, self.b = x, y
+            self.d1, self.d2 = z * 4 + y * 2 + 1 - x, z * 4 + (1 - y) * 2 + x
+    def c1(self):
+        al = slice(None)
+        return rdma(self.sel(al, 1 - self.a, al), self.r1, self.ssem.at[0], self.rsem.at[0], self.d1)
+    def c2(self):
+        return rdma(self.r1.at[:, 1 - self.b], self.r2, self.ssem.at[1], self.rsem.at[1], self.d2)
+    def c3(self, d):
+        zt = lax.rem(self.z + d, 4)
+        return rdma(self.r2.at[zt], self.r3.at[d - 1], self.ssem.at[1 + d], self.rsem.at[1 + d], zt * 4 + self.y * 2 + self.x)
+    def s0(self):
+        self.c1().start()
+    def s1(self):
+        self.c1().wait()
+        o = 1 - self.b
+        def add(zz, _):
+            t = self.r1.at[zz, o]
+            t[...] = (t[...].astype(jnp.float32) + self.sel(zz, self.a, o)[...].astype(jnp.float32)).astype(t.dtype)
+            return 0
+        lax.fori_loop(0, 4, add, 0)
+        self.c2().start()
+    def s2(self):
+        self.c2().wait()
+        def add(d, _):
+            zz = lax.rem(self.z + d, 4)
+            t = self.r2.at[zz]
+            t[...] = (t[...].astype(jnp.float32) + self.r1[zz, self.b].astype(jnp.float32) + self.sel(zz, self.a, self.b)[...].astype(jnp.float32)).astype(t.dtype)
+            return 0
+        lax.fori_loop(1, 4, add, 0)
+        for d in (2, 1, 3): self.c3(d).start()
+    def s3(self):
+        for d in (2, 1, 3): self.c3(d).wait()
+        f = lambda v: v.astype(jnp.float32)
+        z = self.z
+        self.out[...] = f(self.sel(z, self.a, self.b)[...]) + f(self.r1[z, self.b]) + f(self.r2[z]) + f(self.r3[0]) + f(self.r3[1]) + f(self.r3[2])
+
+
+def pipeline(groups, stages):
+    n = len(groups)
+    for s in range(n + stages - 1):
+        for k in range(stages):
+            if 0 <= s - k < n:
+                for flow in groups[s - k]:
+                    getattr(flow, f"s{k}")()
+
+
+def cuts_of(i, rows):
+    if i in (1, 5):
+        return [(0, rows, "x")]
+    if i == 2:
+        return [(0, rows, "y")]
+    return [(0, rows // 32 * 16, "x"), (rows // 32 * 16, rows, "y")]
+
+
+def gather_kernel(*refs):
+    n = 6
+    src, dst = refs[:n], refs[n : 2 * n]
+    ssem, rsem, lsem = refs[2 * n :]
+    enter()
+    fl = []
+    for i, (s, d) in enumerate(zip(src, dst)):
+        for a, b, first in cuts_of(i, s.shape[0]):
+            j = len(fl)
+            fl.append(
+                Gather(
+                    s.at[a:b],
+                    lambda z, y, x, d=d, a=a, b=b: d.at[z, y, x, a:b],
+                    first,
+                    ssem.at[j],
+                    rsem.at[j],
+                    lsem.at[j],
+                )
+            )
+    pipeline([[fl[0], fl[1], fl[8]], [fl[6], fl[7]], [fl[2], fl[3]], [fl[4], fl[5]]], 4)
+
+
+def gather_call(shards_low):
+    n = len(shards_low)
+    return pl.pallas_call(
+        gather_kernel,
+        out_shape=[jax.ShapeDtypeStruct(TORUS + s.shape, s.dtype) for s in shards_low],
+        in_specs=[pl.BlockSpec(memory_space=pltpu.VMEM)] * n,
+        out_specs=[pl.BlockSpec(memory_space=pl.ANY)] * n,
+        scratch_shapes=[
+            pltpu.SemaphoreType.DMA((9, 5)),
+            pltpu.SemaphoreType.DMA((9, 5)),
+            pltpu.SemaphoreType.DMA((9,)),
+        ],
+        compiler_params=pltpu.CompilerParams(
+            collective_id=0, has_side_effects=True, vmem_limit_bytes=60 << 20
+        ),
+    )(*shards_low)
+
+
+def scatter_kernel(*refs):
+    n = 6
+    g, out, r1, r2, r3 = (refs[k * n : (k + 1) * n] for k in range(5))
+    ssem, rsem = refs[5 * n :]
+    enter()
+    fl = []
+    for i in range(n):
+        for a, b, first in cuts_of(i, out[i].shape[0]):
+            j = len(fl)
+            fl.append(
+                Scatter(
+                    lambda z, y, x, i=i, a=a, b=b: g[i].at[z, y, x, a:b],
+                    r1[i].at[:, :, a:b],
+                    r2[i].at[:, a:b],
+                    r3[i].at[:, a:b],
+                    out[i].at[a:b],
+                    first,
+                    ssem.at[j],
+                    rsem.at[j],
+                )
+            )
+    pipeline([[fl[2], fl[3]], [fl[4], fl[5]], [fl[0], fl[1]], [fl[6], fl[7], fl[8]]], 4)
+
+
+def scatter_call(parts):
+    n = len(parts)
+    vmem = pl.BlockSpec(memory_space=pltpu.VMEM)
+    return pl.pallas_call(
+        scatter_kernel,
+        out_shape=[jax.ShapeDtypeStruct(v.shape[3:], jnp.float32) for v in parts],
+        in_specs=[vmem] * n,
+        out_specs=[vmem] * n,
+        scratch_shapes=[pltpu.VMEM((4, 2) + v.shape[3:], v.dtype) for v in parts]
+        + [pltpu.VMEM((4,) + v.shape[3:], v.dtype) for v in parts]
+        + [pltpu.VMEM((3,) + v.shape[3:], v.dtype) for v in parts]
+        + [pltpu.SemaphoreType.DMA((9, 5)), pltpu.SemaphoreType.DMA((9, 5))],
+        compiler_params=pltpu.CompilerParams(
+            collective_id=1, has_side_effects=True, vmem_limit_bytes=60 << 20
+        ),
+    )(*parts)
+
+
+def gather_weights(weight_qkv, weight_out, weight_gate_up, weight_down, head_bias, norm_vectors):
+    n = lax.axis_size("dp")
+    low = lambda v: v.astype(jnp.bfloat16)
+    if n != TORUS[0] * TORUS[1] * TORUS[2]:
+        return (
+            lax.all_gather(low(weight_qkv), "dp", axis=1, tiled=True),
+            lax.all_gather(low(weight_out), "dp", axis=0, tiled=True),
+            lax.all_gather(low(weight_gate_up), "dp", axis=1, tiled=True),
+            lax.all_gather(low(weight_down), "dp", axis=0, tiled=True),
+            lax.all_gather(low(head_bias), "dp", axis=1, tiled=True),
+            lax.all_gather(low(norm_vectors), "dp", axis=1, tiled=True),
+        )
+    me = lax.axis_index("dp")
+    width = weight_qkv.shape[2]
+    model = weight_out.shape[1]
+    rows_out = weight_out.shape[0]
+    qkv = low(weight_qkv).reshape(-1, width)
+    out = jnp.pad(low(weight_out), ((0, -rows_out % 32), (0, 0)))
+    small = jnp.zeros((16, model), jnp.bfloat16)
+    small = lax.dynamic_update_slice(small, low(norm_vectors), (0, me * norm_vectors.shape[1]))
+    small = lax.dynamic_update_slice(small, low(head_bias), (8, me * head_bias.shape[1]))
+    qkv, gate, up, down, out, small = gather_call(
+        [qkv, low(weight_gate_up[0]), low(weight_gate_up[1]), low(weight_down), out, small]
+    )
+    small = jnp.sum(small.reshape(n, 16, model).astype(jnp.float32), axis=0)
+    qkv = qkv.reshape(n, 3, -1, width).transpose(1, 0, 2, 3).reshape(3, model, width)
+    return (
+        qkv,
+        out.reshape(n, -1, model)[:, :rows_out].reshape(-1, model),
+        jnp.stack([gate.reshape(model, -1), up.reshape(model, -1)]),
+        down.reshape(-1, model),
+        small[8:10, :width],
+        small[:6],
+    )
+
+
+def reduce_grads(grad_qkv, grad_out, grad_gate_up, grad_down, grad_heads, grad_vectors):
+    n = lax.axis_size("dp")
+    low = lambda v: v.astype(jnp.bfloat16)
+    if n != TORUS[0] * TORUS[1] * TORUS[2]:
+        return (
+            lax.psum_scatter(grad_qkv, "dp", scatter_dimension=1, tiled=True),
+            lax.psum_scatter(grad_out, "dp", scatter_dimension=0, tiled=True),
+            lax.psum_scatter(grad_gate_up, "dp", scatter_dimension=1, tiled=True),
+            lax.psum_scatter(grad_down, "dp", scatter_dimension=0, tiled=True),
+            lax.psum_scatter(grad_heads, "dp", scatter_dimension=1, tiled=True),
+            lax.psum_scatter(grad_vectors, "dp", scatter_dimension=1, tiled=True),
+        )
+    model, width = grad_qkv.shape[1:]
+    rows = model // n
+    rows_out, rows_heads = grad_out.shape[0] // n, grad_heads.shape[1] // n
+    blocks = lambda v: v.reshape(TORUS + (-1, v.shape[-1]))
+    qkv = blocks(low(grad_qkv).reshape(3, n, rows, width).transpose(1, 0, 2, 3))
+    out = low(grad_out).reshape(n, rows_out, model)
+    out = blocks(jnp.pad(out, ((0, 0), (0, -rows_out % 32), (0, 0))))
+    vec = grad_vectors.reshape(6, n, rows).transpose(1, 0, 2)
+    heads = grad_heads.reshape(2, n, rows_heads).transpose(1, 0, 2)
+    vec = jnp.pad(vec, ((0, 0), (0, 2), (0, 128 - rows)))
+    heads = jnp.pad(heads, ((0, 0), (6, 0), (0, 128 - rows_heads)))
+    qkv, gate, up, down, out, small = scatter_call(
+        [
+            qkv,
+            blocks(low(grad_gate_up[0])),
+            blocks(low(grad_gate_up[1])),
+            blocks(low(grad_down)),
+            out,
+            blocks(vec + heads),
+        ]
+    )
+    return (
+        qkv.reshape(3, rows, width),
+        out[:rows_out],
+        jnp.stack([gate, up]),
+        down,
+        small[6:8, :rows_heads],
+        small[:6, :rows],
+    )
+
+
 def shards(
     inputs,
     segments,
@@ -166,13 +455,8 @@
     head_count = HEADS // lax.axis_size("tensor")
     all_slopes = jnp.asarray(alibi_slopes(HEADS))
     slopes = lax.dynamic_slice_in_dim(all_slopes, lax.axis_index("tensor") * head_count, head_count)
-    proj_qkv, proj_out, proj_gate_up, proj_down, bias_heads, vectors = (
-        lax.all_gather(weight_qkv.astype(jnp.bfloat16), "dp", axis=1, tiled=True),
-        lax.all_gather(weight_out.astype(jnp.bfloat16), "dp", axis=0, tiled=True),
-        lax.all_gather(weight_gate_up.astype(jnp.bfloat16), "dp", axis=1, tiled=True),
-        lax.all_gather(weight_down.astype(jnp.bfloat16), "dp", axis=0, tiled=True),
-        lax.all_gather(head_bias.astype(jnp.bfloat16), "dp", axis=1, tiled=True),
-        lax.all_gather(norm_vectors.astype(jnp.bfloat16), "dp", axis=1, tiled=True),
+    proj_qkv, proj_out, proj_gate_up, proj_down, bias_heads, vectors = gather_weights(
+        weight_qkv, weight_out, weight_gate_up, weight_down, head_bias, norm_vectors
     )
     bias_heads = bias_heads.astype(jnp.float32)
     vectors = vectors.astype(jnp.float32)
@@ -256,13 +540,8 @@
             d_shift_two,
         ]
     )
-    grad_qkv, grad_out, grad_gate_up, grad_down, grad_heads, grad_vectors = (
-        lax.psum_scatter(grad_qkv, "dp", scatter_dimension=1, tiled=True),
-        lax.psum_scatter(grad_out, "dp", scatter_dimension=0, tiled=True),
-        lax.psum_scatter(grad_gate_up, "dp", scatter_dimension=1, tiled=True),
-        lax.psum_scatter(grad_down, "dp", scatter_dimension=0, tiled=True),
-        lax.psum_scatter(grad_heads, "dp", scatter_dimension=1, tiled=True),
-        lax.psum_scatter(grad_vectors, "dp", scatter_dimension=1, tiled=True),
+    grad_qkv, grad_out, grad_gate_up, grad_down, grad_heads, grad_vectors = reduce_grads(
+        grad_qkv, grad_out, grad_gate_up, grad_down, grad_heads, grad_vectors
     )
     second_qkv_new, weight_qkv_new = adam_update(
         weight_qkv, first_qkv, second_qkv, grad_qkv, matrix_rate

time: 1560 us -> 888 us (0.57)
  waiting for transfers between devices: 823 us -> 41.6 us
  Pallas kernels: 0 us -> 234 us
  blocking collectives: 164 us -> 0 us
  other arithmetic: 136 us -> 164 us
    unnamed x13 -> x4, waiting for transfers between devices: 523 us -> 0.07 us
    pallas_call x0 -> x2, Pallas kernels: none -> 234 us  [the longest x1 119 us: gather_call(): pl.pallas_call(gather_kernel, out_shape=[jax.ShapeDtypeStruct(TORUS + s.s...]
    reduce_scatter x2 -> x0, waiting for transfers between devices: 157 us -> none  [the longest x1 141 us: shards(): lax.psum_scatter(grad_down, 'dp', scatter_dimension=0, tiled=True)]
    all_gather x3 -> x0, blocking collectives: 122 us -> none  [the longest x1 42.2 us: shards(): lax.all_gather(weight_out.astype(jnp.bfloat16), 'dp', axis=0, tiled=True)]
    all_gather x3 -> x0, waiting for transfers between devices: 77.3 us -> none  [the longest x1 60.8 us: shards(): lax.all_gather(weight_gate_up.astype(jnp.bfloat16), 'dp', axis=1, tiled=T...]
    broadcast_in_dim x0 -> x2, other arithmetic: none -> 53.9 us  [geglu(): return jax.nn.gelu(gate_up[0], approximate=False) * gate_up[1]]
    unnamed x1 -> x0, blocking collectives: 42 us -> none
    convert_element_type x7 -> x5, other arithmetic: 34.9 us -> 5.69 us  [gather_weights(): low = lambda v: v.astype(jnp.bfloat16)]
  transfers between devices with their start and end apart: 11 -> 4, of which waited for: 9 -> 3; matrix products, arithmetic and copies ran while one was open for 9% -> 9% of each run, Pallas kernels for 0% -> 0%
where the time goes in v1:
time: 888 us; the launch traced here: 879 us
  matrix products  274 us (31%)
  Pallas kernels  234 us (26%)
  other arithmetic  164 us (18%)
  local copies, waits for them, and re-layouts  139 us (16%)
  waiting for transfers between devices  41.6 us (5%)
  between operations  14.8 us (2%)
  loops' own time  11.7 us (1%)
    pallas_call x1, Pallas kernels, gather_call(): pl.pallas_call(gather_kernel, out_shape=[jax.ShapeDtypeStruct(TORUS + s.s...  119 us
    pallas_call x1, Pallas kernels, scatter_call(): pl.pallas_call(scatter_kernel, out_shape=[jax.ShapeDtypeStruct(v.shape[3:...  115 us
    dot_general x8, matrix products, block_scores(): jnp.einsum('qhd,khd->hqk', q_rows, k_seq, preferred_element_type=jnp.floa...  60.1 us
    broadcast_in_dim x2, other arithmetic, geglu(): return jax.nn.gelu(gate_up[0], approximate=False) * gate_up[1]  53.9 us
    dot_general x1, matrix products, shards(): jnp.dot(hidden_low, proj_down, preferred_element_type=jnp.float32)  34.1 us
    dot_general x4, matrix products, one_block(): jnp.einsum('qhd,khd->hqk', dctx_rows, v_seq, preferred_element_type=jnp.f...  30.6 us
    psum x1, waiting for transfers between devices, shards(): lax.psum(ffn_part.astype(jnp.bfloat16), 'tensor').astype(jnp.float32)  24.5 us
    dot_general x1, matrix products, shards(): jnp.einsum('tf,td->fd', hidden_low, d_ffn_low, preferred_element_type=jnp...  22.9 us
  transfers between devices with their start and end apart: 4, of which 3 were waited for; matrix products, arithmetic and copies ran while one was open for 9% of the time, Pallas kernels for 0%

profile of v1, /device:TPU:0, one launch (start us, length us, event | category | flops | bytes accessed | tf_op | source)
XLA Modules:
  0.0 879.3 jit_solution(3514492604521823915)
XLA Ops:
  16.6 118.8 %shard_map.365 = (bf16[4,2,2,144,384]{4,3,2,1,0:T(8,128)(2,1)}, bf16[4,2,2,48,1536]{4,3,2,1,0:T(8,128)(2,1)}, bf16[4,2,2,48,1536]{4,3,2,1,0:T(8,128)(2,1)}, bf16...) custom-call(bf16[144,384]{1,0:T(8,128)(2,1)} %bitcast.328, ...), custom_call_target="tpu_custom_call" | custom-call | tf_op jit(solution)/shard_map/pallas_call | solution.py:295
  161.7 92.6 %while.54 = (s32[]{:T(128)}, bf16[2,1024,6,64]{3,2,1,0:T(8,128)(2,1)}, f32[2,2,6,512]{3,2,1,0:T(8,128)S(1)}, bf16[2,1024,6,64]{1,3,2,0:T(8,128)(2,1)}, s32[2,102...) while((s32[]{:T(128)}, ...), condition=%wide.region_6.7_spmd, body=%wide.region_1.6_spmd.sunk | while | flops 864220672 | bytes 59977184 | solution.py:84
  166.2 38.7 %while.57 = (s32[]{:T(128)}, bf16[2,512,6,64]{1,3,2,0:T(8,128)(2,1)S(1)}, f32[2,6,512]{2,1,0:T(8,128)S(1)}, s32[2]{0:T(128)S(1)}, s32[1024]{0:T(1024)S(1)}, /*in...) while((s32[]{:T(128)}, ...), condition=%wide.region_5.5_spmd, body=%wide.region_2.4_spmd.sunk | while | flops 864220672 | bytes 50728152 | solution.py:81
  170.3 5.8 fusion.194
  212.5 38.7 %while.57 = (s32[]{:T(128)}, bf16[2,512,6,64]{1,3,2,0:T(8,128)(2,1)S(1)}, f32[2,6,512]{2,1,0:T(8,128)S(1)}, s32[2]{0:T(128)S(1)}, s32[1024]{0:T(1024)S(1)}, /*in...) while((s32[]{:T(128)}, ...), condition=%wide.region_5.5_spmd, body=%wide.region_2.4_spmd.sunk | while | flops 864220672 | bytes 50728152 | solution.py:81
  216.5 5.8 fusion.194
  273.3 12.0 %all-reduce.11.cloned.1.call-done = bf16[2048,768]{1,0:T(8,128)(2,1)} async-done(((bf16[2048,768]{1,0:T(8,128)(2,1)}), bf16[2048,768]{1,0:T(8,128)(2,1)}) %all-reduce.11.cloned.1.call-update) | async-done | bytes 3145744 | tf_op jit(solution)/shard_map/psum | solution.py:474
  290.3 15.8 %convolution_bitcast_fusion = f32[2,2048,1536]{1,2,0:T(8,128)} fusion(bf16[1,768,1536]{1,2,0:T(8,128)(2,1)S(1)} %copy-done.21, bf16[1,768,1536]{1,2,0:T(8,128)(2,1)S(1)} %copy-done.19, f32[768]{0:T(1024)S(1)} %get-tuple-element.362, f32[768]{0:T(1024)S(1)} %get-tuple-element.363, f32[2048]{0:T(1024)S(1)} %fusion.90, bf16[2048,768]{1,0:T(8,128)(2,1)S(1)} %copy-done.7, ...), kind=kOutput, calls=%fused_computation.64 | convolution fusion | flops 9680191488 | bytes 36201472 | tf_op jit(solution)/shard_map/td,cdf->ctf/dot_general | solution.py:480
  306.2 34.1 %fusion.74 = bf16[2048,768]{1,0:T(8,128)(2,1)} fusion(bf16[1536,768]{1,0:T(8,128)(2,1)} %bitcast.333, f32[2,2048,1536]{1,2,0:T(8,128)} %convolution_bitcast_fusion), kind=kOutput, calls=%fused_computation.150 | convolution fusion | flops 5041029120 | bytes 30670848 | tf_op jit(solution)/shard_map/dot_general | solution.py:485
  340.4 24.5 %all-reduce.13.cloned.1.call-done = bf16[2048,768]{1,0:T(8,128)(2,1)} async-done(((bf16[2048,768]{1,0:T(8,128)(2,1)}), bf16[2048,768]{1,0:T(8,128)(2,1)}) %all-reduce.13.cloned.1.call-update) | async-done | bytes 3145744 | tf_op jit(solution)/shard_map/psum | solution.py:486
  384.6 30.5 %multiply_bitcast_fusion = (f32[1,2048,1536]{1,2,0:T(8,128)}, f32[2048,1536]{0,1:T(8,128)}) fusion(f32[2048,1536]{0,1:T(8,128)S(1)} %fusion.131, f32[2,2048,1536]{1,2,0:T(8,128)} %convolution_bitcast_fusion), kind=kLoop, calls=%fused_computation.86 | loop fusion | flops 204472320 | bytes 50331648 | tf_op jit(solution)/shard_map/transpose(jvp())/broadcast_in_dim | solution.py:45
  415.1 23.4 %fusion.42 = f32[1,2048,1536]{1,2,0:T(8,128)} fusion(f32[2048,1536]{0,1:T(8,128)} %get-tuple-element.464, f32[2048,1536]{0,1:T(8,128)} %copy-done.11, f32[2,2048,1536]{1,2,0:T(8,128)} %convolution_bitcast_fusion), kind=kLoop, calls=%fused_computation.85 | loop fusion | flops 44040192 | bytes 62914560 | tf_op jit(solution)/shard_map/transpose(jvp())/broadcast_in_dim | solution.py:45
  438.5 16.3 %bitcast_convert_fusion.1 = bf16[2048,768]{1,0:T(8,128)(2,1)} fusion(bf16[1,768,1536]{1,2,0:T(8,128)(2,1)S(1)} %copy-done.22, bf16[1,768,1536]{1,2,0:T(8,128)(2,1)S(1)} %copy-done.20, f32[1,2048,1536]{1,2,0:T(8,128)} %fusion.42, f32[1,2048,1536]{1,2,0:T(8,128)} %get-tuple-element.463), kind=kOutput, calls=%fused_computation.126 | convolution fusion | flops 9680191488 | bytes 33030144 | tf_op jit(solution)/shard_map/ctf,cdf->td/dot_general | solution.py:498
  454.9 19.4 %convert_bitcast_fusion = bf16[2,768,1536]{2,1,0:T(8,128)(2,1)} fusion(f32[1,2048,1536]{1,2,0:T(8,128)} %fusion.42, f32[1,2048,1536]{1,2,0:T(8,128)} %get-tuple-element.463, f32[768]{0:T(1024)S(1)} %get-tuple-element.362, f32[768]{0:T(1024)S(1)} %get-tuple-element.363, f32[2048]{0:T(1024)S(1)} %fusion.90, ...), kind=kOutput, calls=%fused_computation.149 | convolution fusion | flops 9692774400 | bytes 36201472 | tf_op jit(solution)/shard_map/td,ctf->cdf/dot_general | solution.py:495
  479.3 7.7 multiply_reduce_fusion.1
  487.1 6.0 fusion.143
  501.8 157.1 %while.56 = (s32[]{:T(128)}, bf16[2,1024,6,64]{3,2,1,0:T(8,128)(2,1)}, bf16[2,1024,6,64]{1,3,2,0:T(8,128)(2,1)}, bf16[2,1024,6,64]{1,3,2,0:T(8,128)(2,1)}, bf16[...) while((s32[]{:T(128)}, ...), condition=%wide.region_22.23_spmd, body=%wide.region_18.22_spmd.sunk | while | flops 2055271936 | bytes 154279168 | solution.py:134
  513.1 59.1 %while.58 = (s32[]{:T(128)}, f32[1024,6,64]{0,2,1:T(8,128)S(1)}, f32[1024,6,64]{0,2,1:T(8,128)S(1)}, bf16[2,512,6,64]{1,3,2,0:T(8,128)(2,1)}, bf16[2,512,6,64]{1...) while((s32[]{:T(128)}, f32[1024,6,64]{0,2,1:T(8,128)S(1)}, ...), condition=%wide.region_21.21_spmd.clone, body=%wide.region_19.20_spmd.clone.sunk | while | flops 2055271936 | bytes 129579936 | solution.py:129
  515.2 7.7 fusion.190
  522.9 9.3 %multiply_reduce_fusion.6 = (f32[6,512]{1,0:T(8,128)S(1)}, f32[6,512,1024]{2,1,0:T(8,128)S(1)}) fusion(f32[6,512,1024]{2,1,0:T(8,128)} %fusion.190, f32[6,512]{1,0:T(8,128)S(1)} %dynamic-slice_bitcast_fusion.18, f32[512,1024]{1,0:T(8,128)S(1)} %abs_convert_fusion.4, f32[6]{0:T(128)S(1)} %get-tuple-element.843, ...), kind=kOutput, calls=%fused_computation.26.clone.1 | convolution fusion | flops 427815936 | bytes 28996100 | tf_op jit(solution)/shard_map/while/body/eval_jaxpr/while/body/eval_jaxpr/qhd,khd->hqk/dot_general | solution.py:50
  544.8 7.7 fusion.190
  552.4 9.3 %multiply_reduce_fusion.6 = (f32[6,512]{1,0:T(8,128)S(1)}, f32[6,512,1024]{2,1,0:T(8,128)S(1)}) fusion(f32[6,512,1024]{2,1,0:T(8,128)} %fusion.190, f32[6,512]{1,0:T(8,128)S(1)} %dynamic-slice_bitcast_fusion.18, f32[512,1024]{1,0:T(8,128)S(1)} %abs_convert_fusion.4, f32[6]{0:T(128)S(1)} %get-tuple-element.843, ...), kind=kOutput, calls=%fused_computation.26.clone.1 | convolution fusion | flops 427815936 | bytes 28996100 | tf_op jit(solution)/shard_map/while/body/eval_jaxpr/while/body/eval_jaxpr/qhd,khd->hqk/dot_general | solution.py:50
  591.5 59.1 %while.58 = (s32[]{:T(128)}, f32[1024,6,64]{0,2,1:T(8,128)S(1)}, f32[1024,6,64]{0,2,1:T(8,128)S(1)}, bf16[2,512,6,64]{1,3,2,0:T(8,128)(2,1)}, bf16[2,512,6,64]{1...) while((s32[]{:T(128)}, f32[1024,6,64]{0,2,1:T(8,128)S(1)}, ...), condition=%wide.region_21.21_spmd.clone, body=%wide.region_19.20_spmd.clone.sunk | while | flops 2055271936 | bytes 129579936 | solution.py:129
  593.6 7.7 fusion.190
  601.3 9.3 %multiply_reduce_fusion.6 = (f32[6,512]{1,0:T(8,128)S(1)}, f32[6,512,1024]{2,1,0:T(8,128)S(1)}) fusion(f32[6,512,1024]{2,1,0:T(8,128)} %fusion.190, f32[6,512]{1,0:T(8,128)S(1)} %dynamic-slice_bitcast_fusion.18, f32[512,1024]{1,0:T(8,128)S(1)} %abs_convert_fusion.4, f32[6]{0:T(128)S(1)} %get-tuple-element.843, ...), kind=kOutput, calls=%fused_computation.26.clone.1 | convolution fusion | flops 427815936 | bytes 28996100 | tf_op jit(solution)/shard_map/while/body/eval_jaxpr/while/body/eval_jaxpr/qhd,khd->hqk/dot_general | solution.py:50
  623.2 7.7 fusion.190
  630.9 9.3 %multiply_reduce_fusion.6 = (f32[6,512]{1,0:T(8,128)S(1)}, f32[6,512,1024]{2,1,0:T(8,128)S(1)}) fusion(f32[6,512,1024]{2,1,0:T(8,128)} %fusion.190, f32[6,512]{1,0:T(8,128)S(1)} %dynamic-slice_bitcast_fusion.18, f32[512,1024]{1,0:T(8,128)S(1)} %abs_convert_fusion.4, f32[6]{0:T(128)S(1)} %get-tuple-element.843, ...), kind=kOutput, calls=%fused_computation.26.clone.1 | convolution fusion | flops 427815936 | bytes 28996100 | tf_op jit(solution)/shard_map/while/body/eval_jaxpr/while/body/eval_jaxpr/qhd,khd->hqk/dot_general | solution.py:50
  664.9 6.1 reshape.365
  678.3 9.0 %bitcast_convert_fusion = bf16[2048,768]{1,0:T(8,128)(2,1)} fusion(bf16[3,768,384]{2,1,0:T(8,128)(2,1)} %bitcast.321, bf16[1,2048,384]{2,1,0:T(8,128)(2,1)} %copy.94, bf16[1,2048,384]{2,1,0:T(8,128)(2,1)S(1)} %copy.93, bf16[1,2048,384]{2,1,0:T(8,128)(2,1)} %reshape.365), kind=kOutput, calls=%fused_computation.125 | convolution fusion | flops 3630170112 | bytes 9633792 | tf_op jit(solution)/shard_map/ctw,cdw->td/dot_general | solution.py:529
  687.4 22.9 %fusion.77 = bf16[1536,768]{1,0:T(8,128)(2,1)} fusion(f32[2,2048,1536]{1,2,0:T(8,128)} %convolution_bitcast_fusion, f32[2048,1536]{0,1:T(8,128)} %get-tuple-element.464, f32[2048,768]{1,0:T(8,128)} %copy-done.10, f32[2048]{0:T(1024)S(1)} %copy-done.45), kind=kOutput, calls=%fused_computation.151 | convolution fusion | flops 4848746496 | bytes 46407680 | tf_op jit(solution)/shard_map/tf,td->fd/dot_general | solution.py:491
  727.1 7.6 convert_bitcast_fusion.1
  745.3 115.2 %shard_map.366 = (f32[144,384]{1,0:T(8,128)}, f32[48,1536]{1,0:T(8,128)}, f32[48,1536]{1,0:T(8,128)}, f32[96,768]{1,0:T(8,128)}, f32[32,768]{1,0:T(8,128)}, /*index=5*/f32[8,128]{1,0:T(8,128)}) custom-call(bf16[4,2,2,144,384]{4,3,2,1,0:T(8,128)(2,1)} %bitcast.313, bf16[4,2,2,48,1536]{4,3,2,1,0:T(8,128)(2,1)} %bitcast.310, ...), custom_call_target="tpu_custom_call" | custom-call | tf_op jit(solution)/shard_map/pallas_call | solution.py:338
  (391 shorter events, 304.2 us)
Async XLA Ops:
  7.2 133.4 %copy-start.4 = (bf16[2048,768]{1,0:T(8,128)(2,1)S(1)}, bf16[2048,768]{1,0:T(8,128)(2,1)}, u32[]{:S(2)}) copy-start(bf16[2048,768]{1,0:T(8,128)(2,1)} %param.30) | copy-start | bytes 9437188
  7.2 278.1 %all-reduce.11.cloned.1.call-start = ((), (), s32[]{:S(2)}) async-start(), calls=%async_computation | async-start | bytes 6291456 | tf_op jit(solution)/shard_map/psum | solution.py:474
  161.7 97.8 %copy-start.30 = (bf16[16,24,768]{2,1,0:T(8,128)(2,1)S(1)}, bf16[16,24,768]{2,1,0:T(8,128)(2,1)}, u32[]{:S(2)}) copy-start(bf16[16,24,768]{2,1,0:T(8,128)(2,1)} %slice.113) | copy-start | bytes 1769476
  263.1 22.3 %copy-start.5 = (bf16[2048,768]{1,0:T(8,128)(2,1)S(1)}, bf16[2048,768]{1,0:T(8,128)(2,1)}, u32[]{:S(2)}) copy-start(bf16[2048,768]{1,0:T(8,128)(2,1)} %param.30) | copy-start | bytes 9437188
  263.1 101.7 %all-reduce.13.cloned.1.call-start = ((), (), s32[]{:S(2)}) async-start(), calls=%async_computation.1 | async-start | bytes 6291456 | tf_op jit(solution)/shard_map/psum | solution.py:486
  290.3 15.9 %copy-start.48 = (f32[2048]{0:T(1024)}, f32[2048]{0:T(1024)S(1)}, u32[]{:S(2)}) copy-start(f32[2048]{0:T(1024)S(1)} %multiply_reduce_fusion.4) | copy-start | bytes 24580
  340.3 139.1 %all-reduce.15.cloned.1.call-start = ((), (), s32[]{:S(2)}) async-start(), calls=%async_computation.2 | async-start | bytes 6291456 | tf_op jit(solution)/shard_map/psum | solution.py:501
  379.4 107.8 %copy-start.44 = (f32[2048]{0:T(1024)}, f32[2048]{0:T(1024)S(1)}, u32[]{:S(2)}) copy-start(f32[2048]{0:T(1024)S(1)} %negate_multiply_fusion.2) | copy-start | bytes 24580
  384.6 30.5 %copy-start.11 = (f32[2048,1536]{0,1:T(8,128)}, f32[2048,1536]{0,1:T(8,128)S(1)}, u32[]{:S(2)}) copy-start(f32[2048,1536]{0,1:T(8,128)S(1)} %fusion.131) | copy-start | bytes 37748740
  415.1 23.4 %copy-start.20 = (bf16[1,768,1536]{1,2,0:T(8,128)(2,1)S(1)}, bf16[1,768,1536]{1,2,0:T(8,128)(2,1)}, u32[]{:S(2)}) copy-start(bf16[1,768,1536]{1,2,0:T(8,128)(2,1)} %copy.76) | copy-start | bytes 7077892
  415.1 23.4 %copy-start.22 = (bf16[1,768,1536]{1,2,0:T(8,128)(2,1)S(1)}, bf16[1,768,1536]{1,2,0:T(8,128)(2,1)}, u32[]{:S(2)}) copy-start(bf16[1,768,1536]{1,2,0:T(8,128)(2,1)} %copy.77) | copy-start | bytes 7077892
  454.8 284.1 %all-reduce.17.cloned.1.call-start = ((), (), s32[]{:S(2)}) async-start(), calls=%async_computation.3 | async-start | bytes 6291456 | tf_op jit(solution)/shard_map/psum | solution.py:531
  687.3 22.9 %copy-start.53 = (f32[768]{0:T(1024)S(1)}, f32[768]{0:T(1024)}, u32[]{:S(2)}) copy-start(f32[768]{0:T(1024)} %get-tuple-element.354) | copy-start | bytes 9220
  687.4 23.0 %copy-start.52 = (f32[768]{0:T(1024)S(1)}, f32[768]{0:T(1024)}, u32[]{:S(2)}) copy-start(f32[768]{0:T(1024)} %get-tuple-element.358) | copy-start | bytes 9220
  744.4 116.2 %copy-start.60 = (f32[2,24]{1,0:T(2,128)S(1)}, f32[2,24]{1,0:T(2,128)}, u32[]{:S(2)}) copy-start(f32[2,24]{1,0:T(2,128)} %param.45) | copy-start | bytes 580
  744.4 116.2 %copy-start.61 = (f32[2,24]{1,0:T(2,128)S(1)}, f32[2,24]{1,0:T(2,128)}, u32[]{:S(2)}) copy-start(f32[2,24]{1,0:T(2,128)} %param.46) | copy-start | bytes 580
  744.4 116.2 %copy-start.62 = (f32[2,24]{1,0:T(2,128)S(1)}, f32[2,24]{1,0:T(2,128)}, u32[]{:S(2)}) copy-start(f32[2,24]{1,0:T(2,128)} %param.47) | copy-start | bytes 580
  744.4 117.6 %copy-start.57 = (f32[6,48]{1,0:T(8,128)S(1)}, f32[6,48]{1,0:T(8,128)}, u32[]{:S(2)}) copy-start(f32[6,48]{1,0:T(8,128)} %param.48) | copy-start | bytes 3460
  744.4 117.6 %copy-start.58 = (f32[6,48]{1,0:T(8,128)S(1)}, f32[6,48]{1,0:T(8,128)}, u32[]{:S(2)}) copy-start(f32[6,48]{1,0:T(8,128)} %param.49) | copy-start | bytes 3460
  744.4 117.6 %copy-start.59 = (f32[6,48]{1,0:T(8,128)S(1)}, f32[6,48]{1,0:T(8,128)}, u32[]{:S(2)}) copy-start(f32[6,48]{1,0:T(8,128)} %param.50) | copy-start | bytes 3460
  744.4 118.8 %copy-start.29 = (f32[3,48,384]{2,1,0:T(8,128)S(1)}, f32[3,48,384]{2,1,0:T(8,128)}, u32[]{:S(2)}) copy-start(f32[3,48,384]{2,1,0:T(8,128)} %param.33) | copy-start | bytes 663556
  744.4 118.8 %copy-start.40 = (f32[3,48,384]{2,1,0:T(8,128)S(1)}, f32[3,48,384]{2,1,0:T(8,128)}, u32[]{:S(2)}) copy-start(f32[3,48,384]{2,1,0:T(8,128)} %param.34) | copy-start | bytes 663556
  744.4 118.8 %copy-start.41 = (f32[3,48,384]{2,1,0:T(8,128)S(1)}, f32[3,48,384]{2,1,0:T(8,128)}, u32[]{:S(2)}) copy-start(f32[3,48,384]{2,1,0:T(8,128)} %param.35) | copy-start | bytes 663556
  744.4 120.7 %copy-start.26 = (f32[96,768]{1,0:T(8,128)S(1)}, f32[96,768]{1,0:T(8,128)}, u32[]{:S(2)}) copy-start(f32[96,768]{1,0:T(8,128)} %param.42) | copy-start | bytes 884740
  744.5 120.7 %copy-start.37 = (f32[96,768]{1,0:T(8,128)S(1)}, f32[96,768]{1,0:T(8,128)}, u32[]{:S(2)}) copy-start(f32[96,768]{1,0:T(8,128)} %param.43) | copy-start | bytes 884740
  744.5 120.7 %copy-start.38 = (f32[96,768]{1,0:T(8,128)S(1)}, f32[96,768]{1,0:T(8,128)}, u32[]{:S(2)}) copy-start(f32[96,768]{1,0:T(8,128)} %param.44) | copy-start | bytes 884740
  745.3 121.8 %copy-start.39 = (f32[24,768]{1,0:T(8,128)S(1)}, f32[24,768]{1,0:T(8,128)}, u32[]{:S(2)}) copy-start(f32[24,768]{1,0:T(8,128)} %param.36) | copy-start | bytes 221188
  745.3 121.8 %copy-start.50 = (f32[24,768]{1,0:T(8,128)S(1)}, f32[24,768]{1,0:T(8,128)}, u32[]{:S(2)}) copy-start(f32[24,768]{1,0:T(8,128)} %param.37) | copy-start | bytes 221188
  745.3 121.8 %copy-start.51 = (f32[24,768]{1,0:T(8,128)S(1)}, f32[24,768]{1,0:T(8,128)}, u32[]{:S(2)}) copy-start(f32[24,768]{1,0:T(8,128)} %param.38) | copy-start | bytes 221188
  745.3 123.4 %copy-start.23 = (f32[2,48,1536]{2,1,0:T(8,128)S(1)}, f32[2,48,1536]{2,1,0:T(8,128)}, u32[]{:S(2)}) copy-start(f32[2,48,1536]{2,1,0:T(8,128)} %param.39) | copy-start | bytes 1769476
  745.3 123.4 %copy-start.32 = (f32[2,48,1536]{2,1,0:T(8,128)S(1)}, f32[2,48,1536]{2,1,0:T(8,128)}, u32[]{:S(2)}) copy-start(f32[2,48,1536]{2,1,0:T(8,128)} %param.40) | copy-start | bytes 1769476
  745.3 123.4 %copy-start.33 = (f32[2,48,1536]{2,1,0:T(8,128)S(1)}, f32[2,48,1536]{2,1,0:T(8,128)}, u32[]{:S(2)}) copy-start(f32[2,48,1536]{2,1,0:T(8,128)} %param.41) | copy-start | bytes 1769476
  (55 other events, 314.4 us)
Sparse Core Ops, SparseCore 0:
  263.2 22.0 all-reduce.10
  340.4 24.3 all-reduce.12
  454.9 24.3 all-reduce.14
  687.5 24.3 all-reduce.16

commit v2 on v0

v2 whole, which is shorter than its diff:
```python
import functools
import math

import jax
import jax.numpy as jnp
import numpy as np
from jax import lax
from jax.experimental import pallas as pl
from jax.experimental.pallas import tpu as pltpu
from jax.sharding import PartitionSpec as P

HEADS = 12
HEAD_DIM = 64
SEQ = 1024
STEP = 10

norm_epsilon = 1e-12
beta_first = 0.9
beta_second = 0.999
adam_epsilon = 1e-08
decay_rate = 0.1
matrix_rate = 0.05
vector_rate = 0.5

MESH = pl.DeviceIdType.MESH
TORUS = (4, 2, 2)
f32, bf16 = jnp.float32, jnp.bfloat16
LOG2E = 1.4426950408889634
FAR = 3e12
REACH = 512
BQ = 256
TM = 256
HC = 512
VMEM = pl.BlockSpec(memory_space=pltpu.VMEM)
SMEM = pl.BlockSpec(memory_space=pltpu.SMEM)
ANY = pl.BlockSpec(memory_space=pl.ANY)


def alibi_slopes(head_total):
    power_two = 2 ** int(math.floor(math.log2(head_total)))
    leading = [2.0 ** (-8.0 * (h + 1) / power_two) for h in range(power_two)]
    trailing = [
        2.0 ** (-8.0 * (2 * h + 1) / (2 * power_two)) for h in range(head_total - power_two)
    ]
    return np.array(leading + trailing, dtype=np.float32)


def place():
    me = lax.axis_index("dp")
    return lax.div(me, 4), lax.rem(lax.div(me, 2), 2), lax.rem(me, 2)


def chip(z, y, x):
    return z * 4 + y * 2 + x


def remote(src, dst, ssem, rsem, dp):
    return pltpu.make_async_remote_copy(
        src_ref=src,
        dst_ref=dst,
        send_sem=ssem,
        recv_sem=rsem,
        device_id={"dp": dp},
        device_id_type=MESH,
    )


def swap(src, dst, ssem, rsem):
    return pltpu.make_async_remote_copy(
        src_ref=src,
        dst_ref=dst,
        send_sem=ssem,
        recv_sem=rsem,
        device_id={"tensor": 1 - lax.axis_index("tensor")},
        device_id_type=MESH,
    )


def greet(chips, core):
    barrier = pltpu.get_barrier_semaphore()
    count = 0
    if chips:
        z, y, x = place()
        peers = [chip(lax.rem(z + d, 4), y, x) for d in (1, 2, 3)]
        for dp in peers + [chip(z, 1 - y, x), chip(z, y, 1 - x)]:
            pl.semaphore_signal(barrier, inc=1, device_id={"dp": dp}, device_id_type=MESH)
            count += 1
    if core:
        other = {"tensor": 1 - lax.axis_index("tensor")}
        pl.semaphore_signal(barrier, inc=1, device_id=other, device_id_type=MESH)
        count += 1
    pl.semaphore_wait(barrier, count)


class Gather:
    def __init__(self, src, dst, first, ssem, rsem, lsem):
        self.src, self.dst, self.first = src, dst, first
        self.ssem, self.rsem, self.lsem = ssem, rsem, lsem
        self.z, self.y, self.x = place()

    def own(self):
        return pltpu.make_async_copy(self.src, self.dst(self.z, self.y, self.x), self.lsem)

    def along_z(self, d, arriving):
        z, y, x = self.z, self.y, self.x
        other = lax.rem(z + (4 - d if arriving else d), 4)
        slot = self.dst(other if arriving else z, y, x)
        return remote(self.src, slot, self.ssem.at[d - 1], self.rsem.at[d - 1], chip(other, y, x))

    def plane(self, k, arriving):
        z, y, x = self.z, self.y, self.x
        whole = slice(None)
        on_x = (self.first == "x") == (k == 0)
        dp = chip(z, y, 1 - x) if on_x else chip(z, 1 - y, x)
        yy, xx = y, x
        if arriving:
            yy, xx = (y, 1 - x) if on_x else (1 - y, x)
        if k == 1:
            yy, xx = (whole, xx) if on_x else (yy, whole)
        part = self.dst(whole, yy, xx)
        return remote(part, part, self.ssem.at[3 + k], self.rsem.at[3 + k], dp)

    def s0(self):
        self.own().start()
        for d in (1, 3, 2):
            self.along_z(d, False).start()

    def s1(self):
        self.own().wait()
        for d in (1, 3, 2):
            self.along_z(d, False).wait_send()
            self.along_z(d, True).wait_recv()
        self.plane(0, False).start()

    def s2(self):
        self.plane(0, False).wait_send()
        self.plane(0, True).wait_recv()
        self.plane(1, False).start()

    def s3(self):
        self.plane(1, False).wait_send()
        self.plane(1, True).wait_recv()


class Scatter:
    def __init__(self, g, r1, r2, r3, out, first, ssem, rsem):
        self.r1, self.r2, self.r3, self.out, self.ssem, self.rsem = r1, r2, r3, out, ssem, rsem
        z, y, x = self.z, self.y, self.x = place()
        on_y, on_x = chip(z, 1 - y, x), chip(z, y, 1 - x)
        if first == "y":
            self.block = lambda zz, a, b: g(zz, a, b)
            self.a, self.b, self.to1, self.to2 = y, x, on_y, on_x
        else:
            self.block = lambda zz, a, b: g(zz, b, a)
            self.a, self.b, self.to1, self.to2 = x, y, on_x, on_y

    def c1(self):
        whole = slice(None)
        src = self.block(whole, 1 - self.a, whole)
        return remote(src, self.r1, self.ssem.at[0], self.rsem.at[0], self.to1)

    def c2(self):
        src = self.r1.at[:, 1 - self.b]
        return remote(src, self.r2, self.ssem.at[1], self.rsem.at[1], self.to2)

    def c3(self, d):
        to = lax.rem(self.z + d, 4)
        dp = chip(to, self.y, self.x)
        return remote(
            self.r2.at[to], self.r3.at[d - 1], self.ssem.at[1 + d], self.rsem.at[1 + d], dp
        )

    def s0(self):
        self.c1().start()

    def s1(self):
        self.c1().wait()
        o = 1 - self.b

        def add(zz, carry):
            t = self.r1.at[zz, o]
            t[...] = (t[...].astype(f32) + self.block(zz, self.a, o)[...].astype(f32)).astype(t.dtype)
            return carry

        lax.fori_loop(0, 4, add, 0)
        self.c2().start()

    def s2(self):
        self.c2().wait()

        def add(d, carry):
            zz = lax.rem(self.z + d, 4)
            t = self.r2.at[zz]
            here = self.r1[zz, self.b].astype(f32) + self.block(zz, self.a, self.b)[...].astype(f32)
            t[...] = (t[...].astype(f32) + here).astype(t.dtype)
            return carry

        lax.fori_loop(1, 4, add, 0)
        for d in (2, 1, 3):
            self.c3(d).start()

    def s3(self):
        for d in (2, 1, 3):
            self.c3(d).wait()
        z = self.z
        total = self.block(z, self.a, self.b)[...].astype(f32) + self.r1[z, self.b].astype(f32)
        total = total + self.r2[z].astype(f32)
        for d in range(3):
            total = total + self.r3[d].astype(f32)
        self.out[...] = total


def run(flows, stage):
    for flow in flows:
        getattr(flow, f"s{stage}")()


def halves(rows):
    return ((0, rows // 32 * 16, "x"), (rows // 32 * 16, rows, "y"))


def routed():
    return lax.axis_size("dp") == TORUS[0] * TORUS[1] * TORUS[2]


def nt(a, b):
    return lax.dot_general(a, b, (((1,), (1,)), ((), ())), preferred_element_type=f32)


def nn(a, b):
    return jnp.dot(a, b, preferred_element_type=f32)


def span(b, seq):
    lo = max(0, (b * BQ - REACH + 1) // BQ * BQ)
    hi = min(seq, -(-(b * BQ + BQ - 1 + REACH) // BQ) * BQ)
    return lo, hi


def fill_far(far_ref, seg_col, seg_row, seq):
    def rows(c, carry):
        o = pl.multiple_of(c * 128, 128)
        r = lax.broadcasted_iota(jnp.int32, (128, seq), 0) + o
        k = lax.broadcasted_iota(jnp.int32, (128, seq), 1)
        d = jnp.abs(r - k).astype(f32)
        far_ref[pl.ds(o, 128), :] = jnp.where(seg_col[pl.ds(o, 128), :] == seg_row, d, FAR)
        return carry

    lax.fori_loop(0, seq // 128, rows, 0)


def half(value, which):
    lane = lax.broadcasted_iota(jnp.int32, value.shape, 1)
    keep = (lane < 64) if which == 0 else (lane >= 64)
    return jnp.where(keep, value, jnp.zeros_like(value))


def attend_pair(s, pair, q_ref, k_ref, v_ref, vt_ref, far_ref, slope_ref, ctx_ref, lse_ref, seq, pairs):
    cols = pl.ds(pl.multiple_of(pair * 128, 128), 128)
    base = s * seq
    at = lambda lo, n: pl.ds(pl.multiple_of(base + lo, 128), n)
    vt_ref[...] = v_ref[at(0, seq), cols].T
    slopes = [slope_ref[2 * pair + h] for h in range(2)]
    for b in range(seq // BQ):
        lo, hi = span(b, seq)
        qb = q_ref[at(b * BQ, BQ), cols] * jnp.asarray(HEAD_DIM**-0.5, bf16)
        kb = k_ref[at(lo, hi - lo), cols]
        far = lambda: far_ref[lo:hi, b * BQ : (b + 1) * BQ]
        score = [nt(kb, half(qb, h)) * LOG2E - slopes[h] * far() for h in range(2)]
        top = [jnp.max(t, axis=0, keepdims=True) for t in score]
        weight = [jnp.exp2(t - m) for t, m in zip(score, top)]
        total = [jnp.sum(e, axis=0, keepdims=True) for e in weight]
        out = [
            nn(vt_ref[64 * h : 64 * h + 64, lo:hi], weight[h].astype(bf16)) * (1.0 / total[h])
            for h in range(2)
        ]
        for h in range(2):
            lse_ref[s * pairs + pair, h : h + 1, b * BQ : (b + 1) * BQ] = top[h] + jnp.log2(total[h])
        ctx_ref[at(b * BQ, BQ), cols] = jnp.concatenate(out, axis=0).T.astype(bf16)


def attend_pair_back(
    s, pair, q_ref, k_ref, v_ref, ctx_ref, dctx_ref, lse_ref, far_ref, slope_ref,
    kt_ref, dk_acc, dv_acc, dq_ref, dk_ref, dv_ref, seq, pairs,
):
    cols = pl.ds(pl.multiple_of(pair * 128, 128), 128)
    base = s * seq
    at = lambda lo, n: pl.ds(pl.multiple_of(base + lo, 128), n)
    kt_ref[...] = k_ref[at(0, seq), cols].T
    slopes = [slope_ref[2 * pair + h] for h in range(2)]
    dk_acc[...] = jnp.zeros_like(dk_acc)
    dv_acc[...] = jnp.zeros_like(dv_acc)
    for b in range(seq // BQ):
        lo, hi = span(b, seq)
        qb = q_ref[at(b * BQ, BQ), cols] * jnp.asarray(HEAD_DIM**-0.5, bf16)
        db = dctx_ref[at(b * BQ, BQ), cols]
        prod = (db.astype(f32) * ctx_ref[at(b * BQ, BQ), cols].astype(f32)).T
        out = []
        for h in range(2):
            qh, dh = half(qb, h), half(db, h)
            delta = jnp.sum(prod[64 * h : 64 * h + 64], axis=0, keepdims=True)
            lse = lse_ref[s * pairs + pair, h : h + 1, b * BQ : (b + 1) * BQ]
            score = nt(k_ref[at(lo, hi - lo), cols], qh) * LOG2E
            p = jnp.exp2(score - slopes[h] * far_ref[lo:hi, b * BQ : (b + 1) * BQ] - lse)
            ds = (p * (nt(v_ref[at(lo, hi - lo), cols], dh) - delta)).astype(bf16)
            dv_acc[lo:hi, :] += nn(p.astype(bf16), dh)
            dk_acc[lo:hi, :] += nn(ds, qh)
            out.append(nn(kt_ref[64 * h : 64 * h + 64, lo:hi], ds))
        dq = jnp.concatenate(out, axis=0).T * HEAD_DIM**-0.5
        dq_ref[at(b * BQ, BQ), cols] = dq.astype(bf16)
    dk_ref[at(0, seq), cols] = dk_acc[...].astype(bf16)
    dv_ref[at(0, seq), cols] = dv_acc[...].astype(bf16)


def front_kernel(*refs, seq, pairs, routes):
    n = 4 if routes else 0
    x_ref, segc_ref, segr_ref, slope_ref, qkv_in, small_in = refs[:6]
    sources, refs = refs[6 : 6 + n], refs[6 + n :]
    q_ref, k_ref, v_ref, ctx_ref, lse_ref, small_ref = refs[:6]
    outs, refs = refs[6 : 6 + n], refs[6 + n :]
    if routes:
        w_out, refs = refs[0], refs[1:]
    far_ref, vt_ref = refs[:2]
    rows, width = x_ref.shape[0], q_ref.shape[1]
    model = x_ref.shape[1]
    if routes:
        w_ref, sm_ref, ssem, rsem, lsem, w_sem = refs[2:]
        greet(True, False)
        flows = []

        def flow(src, dst, cuts):
            made = []
            for a, b, first in cuts:
                j = len(flows)
                slot = lambda z, y, x, a=a, b=b: dst.at[z, y, x, a:b]
                made.append(Gather(src.at[a:b], slot, first, ssem.at[j], rsem.at[j], lsem.at[j]))
                flows.append(made[-1])
            return made

        whole = lambda s, first: ((0, s.shape[0], first),)
        gate, up, down, out = sources
        lead = flow(qkv_in, w_ref, halves(qkv_in.shape[0])) + flow(small_in, sm_ref, whole(small_in, "x"))
        second = flow(down, outs[2], halves(down.shape[0])) + flow(out, outs[3], halves(out.shape[0]))
        third = flow(gate, outs[0], whole(gate, "x")) + flow(up, outs[1], whole(up, "y"))
        run(lead, 0)
        run(lead, 1)
        run(second, 0)
        run(lead, 2)
        run(lead, 3)
        run(second, 1)
        run(third, 0)
        keep = pltpu.make_async_copy(w_ref, w_out, w_sem)
        keep.start()
        blocks = TORUS[0] * TORUS[1] * TORUS[2]
        load_w = lambda a, b: w_ref[:, :, :, a:b, :]
        small = sum(
            sm_ref[z, y, x].astype(f32)
            for z in range(TORUS[0])
            for y in range(TORUS[1])
            for x in range(TORUS[2])
        )
    else:
        blocks = 1
        load_w = lambda a, b: qkv_in[:, a:b, :]
        small = small_in[0].astype(f32)
    small_ref[...] = small
    each = model // blocks

    def project(i, carry):
        at = pl.ds(pl.multiple_of(i * TM, TM), TM)
        xb = x_ref[at, :]
        for j, (ref, bias) in enumerate(((q_ref, 8), (k_ref, None), (v_ref, 9))):
            val = nn(xb, load_w(j * each, (j + 1) * each).reshape(model, width))
            if bias is not None:
                val = val + small[bias : bias + 1, :width]
            ref[at, :] = val.astype(bf16)
        return carry

    lax.fori_loop(0, rows // TM, project, 0)
    total = segr_ref.shape[0] * pairs

    def step(it, carry):
        s, pair = lax.div(it, pairs), lax.rem(it, pairs)

        @pl.when(pair == 0)
        def _():
            fill_far(far_ref, segc_ref.at[s], segr_ref[s], seq)

        attend_pair(
            s, pair, q_ref, k_ref, v_ref, vt_ref, far_ref, slope_ref, ctx_ref, lse_ref, seq, pairs
        )
        if routes:

            @pl.when(it == 0)
            def _():
                run(second, 2)

            @pl.when(it == total - 2)
            def _():
                run(third, 1)

        return carry

    lax.fori_loop(0, total, step, 0)
    if routes:
        run(second, 3)
        run(third, 2)
        run(third, 3)
        keep.wait()


def front(x, segments, slopes, qkv, small, sources):
    routes = routed()
    rows, width = x.shape[0], qkv.shape[-1]
    count, seq = segments.shape
    pairs = width // 128
    low = lambda *s: jax.ShapeDtypeStruct(s, bf16)
    full = lambda *s: jax.ShapeDtypeStruct(s, f32)
    outs = [low(rows, width)] * 4 + [full(count * pairs, 8, seq), full(*small.shape[-2:])]
    scratch = [pltpu.VMEM((seq, seq), f32), pltpu.VMEM((128, seq), bf16)]
    params = pltpu.CompilerParams(vmem_limit_bytes=56 << 20)
    if routes:
        outs += [low(*TORUS, *s.shape) for s in [*sources, qkv]]
        scratch += [pltpu.VMEM(TORUS + qkv.shape, bf16), pltpu.VMEM(TORUS + small.shape, bf16)]
        dma = pltpu.SemaphoreType.DMA
        scratch += [dma((9, 5)), dma((9, 5)), dma((9,)), dma]
        params = pltpu.CompilerParams(
            vmem_limit_bytes=56 << 20, collective_id=0, has_side_effects=True
        )
    return pl.pallas_call(
        functools.partial(front_kernel, seq=seq, pairs=pairs, routes=routes),
        out_shape=outs,
        in_specs=[VMEM, VMEM, VMEM, SMEM, VMEM, VMEM] + [VMEM] * len(sources),
        out_specs=[VMEM] * 6 + [ANY] * (len(outs) - 6),
        scratch_shapes=scratch,
        compiler_params=params,
        name="front",
    )(x, segments[..., None], segments[:, None, :], slopes * LOG2E, qkv, small, *sources)


def stats(h):
    mean = jnp.mean(h, axis=-1, keepdims=True)
    c = h - mean
    r = lax.rsqrt(jnp.mean(c * c, axis=-1, keepdims=True) + norm_epsilon)
    return c * r, r

def norm_back(e, n, r):
    return r * (e - jnp.mean(e, axis=-1, keepdims=True) - n * jnp.mean(e * n, axis=-1, keepdims=True))

def mid_kernel(ctx_ref, wo_in, wg_ref, wu_ref, wd_ref, vec_ref, x_hbm, cot_hbm,
               out_hbm, dattn_hbm, dctx_ref, dwg_hbm, dwu_hbm, dwd_hbm, dwo_ref, dvec_ref,
               wo_ref, io, s1, q1, s2, q2, n1, rr, xt, ht, av, bv, wide, tall,
               io_sem, out_sem, dat_sem, ssem, rsem, wsem, *, tiles, ff):
    n_blk, wide_rows, model = wo_in.shape
    each = ctx_ref.shape[1] // n_blk
    wo_ref[...] = wo_in[:, :each].astype(f32).reshape(n_blk * each, model).astype(bf16)
    bo, bd, g1, c1, g2, c2 = (vec_ref[k:k + 1, :] for k in range(6))
    at = lambda i: pl.ds(pl.multiple_of(i * TM, TM), TM)
    load = lambda hbm, i: pltpu.make_async_copy(hbm.at[at(i)], io.at[at(i)], io_sem.at[i])
    exch = lambda k, i: swap((s1, s2, s1)[k].at[at(i)], (q1, q2, q1)[k].at[at(i)], ssem.at[k, i], rsem.at[k, i])

    def pre(i, _):
        load(x_hbm, i).start()
        return 0
    lax.fori_loop(0, tiles, pre, 0)
    dvec_ref[...] = jnp.zeros_like(dvec_ref)
    greet(False, True)

    def phase_a(i, _):
        s1[at(i), :] = nn(ctx_ref[at(i), :], wo_ref[...]).astype(bf16)
        exch(0, i).start()
        return 0
    lax.fori_loop(0, tiles, phase_a, 0)

    def phase_b(i, _):
        exch(0, i).wait()
        load(x_hbm, i).wait()
        attn = s1[at(i), :].astype(f32) + q1[at(i), :].astype(f32) + bo
        n, r = stats(io[at(i), :].astype(f32) + attn)
        load(cot_hbm, i).start()
        n1[at(i), :] = n
        rr[at(i), :] = r
        xb = (n * g1 + c1).astype(bf16)
        xt[:, at(i)] = xb.T
        part = None
        for c in range(0, ff, HC):
            gate = nn(xb, wg_ref[:, c:c + HC])
            up = nn(xb, wu_ref[:, c:c + HC])
            cdf = 0.5 * (1.0 + lax.erf(gate * 0.7071067811865476))
            gel = gate * cdf
            slope = cdf + gate * (jnp.exp(gate * gate * -0.5) * 0.3989422804014327)
            hid = (gel * up).astype(bf16)
            ht[c:c + HC, at(i)] = hid.T
            av[at(i), c:c + HC] = (up * slope).astype(bf16)
            bv[at(i), c:c + HC] = gel.astype(bf16)
            p = nn(hid, wd_ref[c:c + HC, :])
            part = p if part is None else part + p
        s2[at(i), :] = part.astype(bf16)
        exch(1, i).start()
        return 0
    lax.fori_loop(0, tiles, phase_b, 0)

    def phase_c(i, _):
        exch(1, i).wait()
        load(cot_hbm, i).wait()
        ffn = s2[at(i), :].astype(f32) + q2[at(i), :].astype(f32) + bd
        n2, r2 = stats(n1[at(i), :] * g1 + c1 + ffn)
        dy = io[at(i), :].astype(f32)
        io[at(i), :] = (n2 * g2 + c2).astype(bf16)
        pltpu.make_async_copy(io.at[at(i)], out_hbm.at[at(i)], out_sem.at[i]).start()
        dvec_ref[4:5, :] += jnp.sum(dy * n2, axis=0, keepdims=True)
        dvec_ref[5:6, :] += jnp.sum(dy, axis=0, keepdims=True)
        dh2 = norm_back(dy * g2, n2, r2)
        dvec_ref[1:2, :] += jnp.sum(dh2, axis=0, keepdims=True)
        df = dh2.astype(bf16)
        s2[at(i), :] = df
        part = None
        for c in range(0, ff, HC):
            dh = nt(df, wd_ref[c:c + HC, :])
            dg = (dh * av[at(i), c:c + HC].astype(f32)).astype(bf16)
            du = (dh * bv[at(i), c:c + HC].astype(f32)).astype(bf16)
            av[at(i), c:c + HC] = dg
            bv[at(i), c:c + HC] = du
            p = nt(dg, wg_ref[:, c:c + HC]) + nt(du, wu_ref[:, c:c + HC])
            part = p if part is None else part + p
        s1[at(i), :] = part.astype(bf16)
        exch(2, i).start()
        return 0
    lax.fori_loop(0, tiles, phase_c, 0)

    def grad_block(left, right, buf, hbm, sem, c, slot, before):
        cols = pl.ds(pl.multiple_of(c * 256, 256), 256)
        val = nn(left[...], right[:, cols]).astype(bf16)
        cp = pltpu.make_async_copy(buf.at[slot], hbm.at[:, cols], sem.at[slot])
        @pl.when(before)
        def _():
            cp.wait()
        buf[slot] = val
        cp.start()
    def e_down(c, _):
        grad_block(ht, s2, tall, dwd_hbm, wsem.at[0], c, lax.rem(c, 2), c >= 2)
        return 0
    nd = s2.shape[1] // 256
    lax.fori_loop(0, nd, e_down, 0)
    def e_gate(c, _):
        grad_block(xt, av, wide, dwg_hbm, wsem.at[1], c, 0, c >= 1)
        grad_block(xt, bv, wide, dwu_hbm, wsem.at[1], c, 1, c >= 1)
        return 0
    nf = ff // 256
    lax.fori_loop(0, nf, e_gate, 0)

    def phase_d(i, _):
        exch(2, i).wait()
        n, r = n1[at(i), :], rr[at(i), :]
        dx1 = s2[at(i), :].astype(f32) + s1[at(i), :].astype(f32) + q1[at(i), :].astype(f32)
        dvec_ref[2:3, :] += jnp.sum(dx1 * n, axis=0, keepdims=True)
        dvec_ref[3:4, :] += jnp.sum(dx1, axis=0, keepdims=True)
        dh1 = norm_back(dx1 * g1, n, r)
        dvec_ref[0:1, :] += jnp.sum(dh1, axis=0, keepdims=True)
        da = dh1.astype(bf16)
        pltpu.make_async_copy(io.at[at(i)], out_hbm.at[at(i)], out_sem.at[i]).wait()
        io[at(i), :] = da
        pltpu.make_async_copy(io.at[at(i)], dattn_hbm.at[at(i)], dat_sem.at[i]).start()
        dctx_ref[at(i), :] = nt(da, wo_ref[...]).astype(bf16)
        return 0
    lax.fori_loop(0, tiles, phase_d, 0)
    dwo = nn(ctx_ref[...].T, io[...])
    dwo_ref[...] = jnp.zeros_like(dwo_ref)
    for b in range(n_blk):
        dwo_ref[b, :each, :] = dwo[b * each : (b + 1) * each].astype(bf16)
    def fin(i, _):
        pltpu.make_async_copy(io.at[at(i)], dattn_hbm.at[at(i)], dat_sem.at[i]).wait()
        return 0
    lax.fori_loop(0, tiles, fin, 0)
    for slot in range(min(2, nd)):
        pltpu.make_async_copy(tall.at[slot], dwd_hbm.at[:, 0:256], wsem.at[0, slot]).wait()
    pltpu.make_async_copy(wide.at[0], dwg_hbm.at[:, 0:256], wsem.at[1, 0]).wait()
    pltpu.make_async_copy(wide.at[1], dwu_hbm.at[:, 0:256], wsem.at[1, 1]).wait()

def middle(ctx, wo, wg, wu, wd, vec, x, cot):
    T, W = ctx.shape
    D, ff, tiles = x.shape[1], wg.shape[1], T // TM
    n_blk, pad = wo.shape[:2]
    sd = lambda *s: jax.ShapeDtypeStruct(s, bf16)
    return pl.pallas_call(functools.partial(mid_kernel, tiles=tiles, ff=ff),
        out_shape=[sd(T, D), sd(T, D), sd(T, W), sd(D, ff), sd(D, ff), sd(ff, D), sd(n_blk, pad, D), jax.ShapeDtypeStruct((8, D), f32)],
        in_specs=[VMEM, VMEM, VMEM, VMEM, VMEM, VMEM, ANY, ANY],
        out_specs=[ANY, ANY, VMEM, ANY, ANY, ANY, VMEM, VMEM],
        scratch_shapes=[pltpu.VMEM((W, D), bf16)] + [pltpu.VMEM((T, D), bf16)] * 5 + [pltpu.VMEM((T, D), f32), pltpu.VMEM((T, 1), f32), pltpu.VMEM((D, T), bf16), pltpu.VMEM((ff, T), bf16), pltpu.VMEM((T, ff), bf16), pltpu.VMEM((T, ff), bf16),
            pltpu.VMEM((2, D, 256), bf16), pltpu.VMEM((2, ff, 256), bf16)]
            + [pltpu.SemaphoreType.DMA((tiles,))] * 3 + [pltpu.SemaphoreType.DMA((3, tiles))] * 2 + [pltpu.SemaphoreType.DMA((2, 2))],
        compiler_params=pltpu.CompilerParams(collective_id=2, has_side_effects=True, vmem_limit_bytes=64 << 20), name="middle")(ctx, wo, wg, wu, wd, vec, x, cot)


def back_kernel(*refs, seq, pairs, routes):
    q_ref, k_ref, v_ref, ctx_ref, dctx_ref, lse_ref, segc_ref, segr_ref, slope_ref = refs[:9]
    x_ref, dh1_ref, w_ref, vec_ref = refs[9:13]
    refs = refs[13:]
    n = 4 if routes else 0
    grads, refs = refs[:n], refs[n:]
    dx_ref = refs[0]
    outs, refs = refs[1 : 1 + n + 2], refs[1 + n + 2 :]
    far_ref, kt_ref, dk_acc, dv_acc, dq_ref, dk_ref, dv_ref, xt, s, r, dx_sem, core_s, core_r = refs[:13]
    refs = refs[13:]
    rows, model = x_ref.shape
    width = q_ref.shape[1]
    tiles = rows // TM
    at = lambda i: pl.ds(pl.multiple_of(i * TM, TM), TM)
    if routes:
        gq, gs, ssem, rsem = refs[:4]
        bufs = refs[4:]
        blocks = TORUS[0] * TORUS[1] * TORUS[2]
        flows = []

        def flow(i, g, cuts):
            r1, r2, r3 = bufs[3 * i : 3 * i + 3]
            made = []
            for a, b, first in cuts:
                j = len(flows)
                flows.append(
                    Scatter(
                        lambda z, y, x, a=a, b=b: g.at[z, y, x, a:b],
                        r1.at[:, :, a:b],
                        r2.at[:, a:b],
                        r3.at[:, a:b],
                        outs[i].at[a:b],
                        first,
                        ssem.at[j],
                        rsem.at[j],
                    )
                )
                made.append(flows[-1])
            return made

        whole = lambda g, first: ((0, g.shape[3], first),)
        split = lambda g: halves(g.shape[3])
        first = flow(0, grads[0], whole(grads[0], "x")) + flow(1, grads[1], whole(grads[1], "y"))
        second = flow(2, grads[2], split(grads[2])) + flow(3, grads[3], split(grads[3]))
        third = flow(4, gq, split(gq)) + flow(5, gs, whole(gs, "x"))
    else:
        blocks = 1
    greet(routes, True)
    if routes:
        run(first, 0)
    total = segr_ref.shape[0] * pairs

    def step(it, carry):
        seq_at, pair = lax.div(it, pairs), lax.rem(it, pairs)

        @pl.when(pair == 0)
        def _():
            fill_far(far_ref, segc_ref.at[seq_at], segr_ref[seq_at], seq)

        attend_pair_back(
            seq_at, pair, q_ref, k_ref, v_ref, ctx_ref, dctx_ref, lse_ref, far_ref, slope_ref,
            kt_ref, dk_acc, dv_acc, dq_ref, dk_ref, dv_ref, seq, pairs,
        )
        if routes:

            @pl.when(it == 2)
            def _():
                run(second, 0)

            @pl.when(it == total - 2)
            def _():
                run(first, 1)

        return carry

    lax.fori_loop(0, total, step, 0)
    each = model // blocks
    if routes:
        load_w = lambda j: w_ref[:, :, :, j * each : (j + 1) * each, :].reshape(model, width)
    else:
        load_w = lambda j: w_ref[:, j * each : (j + 1) * each, :].reshape(model, width)
    d_refs = (dq_ref, dk_ref, dv_ref)
    exch = lambda i: swap(s.at[at(i)], r.at[at(i)], core_s.at[i], core_r.at[i])

    def part(i, carry):
        val = sum(nt(d[at(i), :], load_w(j)) for j, d in enumerate(d_refs))
        s[at(i), :] = val.astype(bf16)
        exch(i).start()
        xt[:, at(i)] = x_ref[at(i), :].T
        return carry

    lax.fori_loop(0, tiles, part, 0)
    heads = [jnp.sum(d[...].astype(f32), axis=0, keepdims=True) for d in (dq_ref, dv_ref)]
    heads = jnp.concatenate([jnp.zeros((6, width), f32)] + heads, axis=0)
    for j, d in enumerate(d_refs):
        val = nn(xt[...], d[...]).astype(bf16)
        for b in range(blocks):
            piece = val[b * each : (b + 1) * each]
            if routes:
                gq[b // 4, (b // 2) % 2, b % 2, j * each : (j + 1) * each, :] = piece
            else:
                outs[0][b, j * each : (j + 1) * each, :] = piece
    if routes:
        share = width // blocks
        row = lax.broadcasted_iota(jnp.int32, (8, 128), 0)
        for b in range(blocks):
            upper = pltpu.roll(vec_ref[...], (model - b * each) % model, 1)[:, :128]
            lower = pltpu.roll(heads, (width - b * share) % width, 1)[:, :128]
            gs[b // 4, (b // 2) % 2, b % 2] = jnp.where(row < 6, upper, lower)
        run(third, 0)
        run(second, 1)
    else:
        outs[1][...] = heads

    def finish(i, carry):
        exch(i).wait()
        val = dh1_ref[at(i), :].astype(f32) + (s[at(i), :].astype(f32) + r[at(i), :].astype(f32))
        s[at(i), :] = val.astype(bf16)
        pltpu.make_async_copy(s.at[at(i)], dx_ref.at[at(i)], dx_sem.at[i]).start()
        return carry

    lax.fori_loop(0, tiles, finish, 0)
    if routes:
        run(first, 2)
        run(third, 1)
        run(second, 2)
        run(first, 3)
        run(third, 2)
        run(second, 3)
        run(third, 3)

    def done(i, carry):
        pltpu.make_async_copy(s.at[at(i)], dx_ref.at[at(i)], dx_sem.at[i]).wait()
        return carry

    lax.fori_loop(0, tiles, done, 0)


def back(q, k, v, ctx, dctx, lse, segments, slopes, x, dh1, w, vec, grads):
    routes = routed()
    rows, width = q.shape
    model = x.shape[1]
    count, seq = segments.shape
    pairs = width // 128
    tiles = rows // TM
    dma = pltpu.SemaphoreType.DMA
    outs = [jax.ShapeDtypeStruct((rows, model), bf16)]
    scratch = [
        pltpu.VMEM((seq, seq), f32),
        pltpu.VMEM((128, seq), bf16),
        pltpu.VMEM((seq, 128), f32),
        pltpu.VMEM((seq, 128), f32),
        pltpu.VMEM((rows, width), bf16),
        pltpu.VMEM((rows, width), bf16),
        pltpu.VMEM((rows, width), bf16),
        pltpu.VMEM((model, rows), bf16),
        pltpu.VMEM((rows, model), bf16),
        pltpu.VMEM((rows, model), bf16),
        dma((tiles,)),
        dma((tiles,)),
        dma((tiles,)),
    ]
    if routes:
        small = (8, 128)
        shapes = [(g.shape[3:], bf16) for g in grads] + [(w.shape[3:], bf16), (small, f32)]
        outs += [jax.ShapeDtypeStruct(sh, f32) for sh, _ in shapes]
        scratch += [pltpu.VMEM(w.shape, bf16), pltpu.VMEM(TORUS + small, f32), dma((9, 5)), dma((9, 5))]
        for sh, dtype in shapes:
            scratch += [
                pltpu.VMEM((4, 2) + sh, dtype),
                pltpu.VMEM((4,) + sh, dtype),
                pltpu.VMEM((3,) + sh, dtype),
            ]
    else:
        outs += [jax.ShapeDtypeStruct(w.shape, bf16), jax.ShapeDtypeStruct((8, width), f32)]
    return pl.pallas_call(
        functools.partial(back_kernel, seq=seq, pairs=pairs, routes=routes),
        out_shape=outs,
        in_specs=[VMEM] * 8 + [SMEM] + [VMEM] * (4 + len(grads)),
        out_specs=[ANY] + [VMEM] * (len(outs) - 1),
        scratch_shapes=scratch,
        compiler_params=pltpu.CompilerParams(
            vmem_limit_bytes=64 << 20, collective_id=1, has_side_effects=True
        ),
        name="back",
    )(q, k, v, ctx, dctx, lse, segments[..., None], segments[:, None, :], slopes * LOG2E, x, dh1, w, vec, *grads)


def adam_update(weight_old, first_old, second_old, gradient, step_rate):
    first_new = beta_first * first_old + (1.0 - beta_first) * gradient
    second_new = beta_second * second_old + (1.0 - beta_second) * gradient * gradient
    first_hat = first_new / (1.0 - beta_first**STEP)
    second_hat = second_new / (1.0 - beta_second**STEP)
    weight_new = weight_old - step_rate * (
        first_hat / (jnp.sqrt(second_hat) + adam_epsilon) + decay_rate * weight_old
    )
    return (second_new, weight_new)


def shards(
    inputs,
    segments,
    cotangent,
    weight_qkv,
    first_qkv,
    second_qkv,
    weight_out,
    first_out,
    second_out,
    weight_gate_up,
    first_gate_up,
    second_gate_up,
    weight_down,
    first_down,
    second_down,
    head_bias,
    first_head_bias,
    second_head_bias,
    norm_vectors,
    first_norm_vectors,
    second_norm_vectors,
):
    head_count = HEADS // lax.axis_size("tensor")
    all_slopes = jnp.asarray(alibi_slopes(HEADS))
    slopes = lax.dynamic_slice_in_dim(all_slopes, lax.axis_index("tensor") * head_count, head_count)
    low = lambda v: v.astype(bf16)
    model, width = weight_out.shape[1], weight_qkv.shape[2]
    rows_out = weight_out.shape[0]
    small = jnp.zeros((16, model), bf16)
    if routed():
        me = lax.axis_index("dp")
        small = lax.dynamic_update_slice(
            small, low(norm_vectors), (0, me * norm_vectors.shape[1])
        )
        small = lax.dynamic_update_slice(small, low(head_bias), (8, me * head_bias.shape[1]))
        qkv = low(weight_qkv).reshape(-1, width)
        sources = [
            low(weight_gate_up[0]),
            low(weight_gate_up[1]),
            low(weight_down),
            jnp.pad(low(weight_out), ((0, -rows_out % 32), (0, 0))),
        ]
        q, k, v, ctx, lse, vec, gate, up, down, out, qkv = front(
            inputs, segments, slopes, qkv, small, sources
        )
        gate, up = gate.reshape(model, -1), up.reshape(model, -1)
        down = down.reshape(-1, model)
        out = out.reshape((-1,) + out.shape[3:])
    else:
        whole = lambda v, axis: lax.all_gather(low(v), "dp", axis=axis, tiled=True)
        qkv = whole(weight_qkv, 1).reshape(1, -1, width)
        out, down = whole(weight_out, 0)[None], whole(weight_down, 0)
        gate, up = whole(weight_gate_up, 1)
        small = small.at[:6].set(whole(norm_vectors, 1)).at[8:10, :width].set(whole(head_bias, 1))
        q, k, v, ctx, lse, vec = front(inputs, segments, slopes, qkv, small[None], [])
    layer_out, dh1, dctx, d_gate, d_up, d_down, d_out, d_vec = middle(
        ctx, out, gate, up, down, vec, inputs, cotangent
    )
    if routed():
        blocks = lambda v: v.reshape(TORUS + (-1, v.shape[-1]))
        grads = [blocks(d_gate), blocks(d_up), blocks(d_down), blocks(d_out)]
        input_grad, d_gate, d_up, grad_down, d_out, d_qkv, d_small = back(
            q, k, v, ctx, dctx, lse, segments, slopes, inputs, dh1, qkv, d_vec, grads
        )
        grad_qkv = d_qkv.reshape(weight_qkv.shape)
        grad_out = d_out[:rows_out]
        grad_gate_up = jnp.stack([d_gate, d_up])
        grad_heads = d_small[6:8, : head_bias.shape[1]]
        grad_vectors = d_small[:6, : norm_vectors.shape[1]]
    else:
        input_grad, d_qkv, d_heads = back(
            q, k, v, ctx, dctx, lse, segments, slopes, inputs, dh1, qkv, d_vec, []
        )
        owned = lambda v, axis: lax.psum_scatter(
            v.astype(f32), "dp", scatter_dimension=axis, tiled=True
        )
        grad_qkv = owned(d_qkv.reshape(3, model, width), 1)
        grad_out = owned(d_out[0], 0)
        grad_gate_up = owned(jnp.stack([d_gate, d_up]), 1)
        grad_down = owned(d_down, 0)
        grad_heads = owned(d_heads[6:8], 1)
        grad_vectors = owned(d_vec[:6], 1)
    second_qkv_new, weight_qkv_new = adam_update(
        weight_qkv, first_qkv, second_qkv, grad_qkv, matrix_rate
    )
    second_out_new, weight_out_new = adam_update(
        weight_out, first_out, second_out, grad_out, matrix_rate
    )
    second_gu_new, weight_gu_new = adam_update(
        weight_gate_up, first_gate_up, second_gate_up, grad_gate_up, matrix_rate
    )
    second_down_new, weight_down_new = adam_update(
        weight_down, first_down, second_down, grad_down, matrix_rate
    )
    second_heads_new, weight_heads_new = adam_update(
        head_bias, first_head_bias, second_head_bias, grad_heads, vector_rate
    )
    second_vectors_new, weight_vectors_new = adam_update(
        norm_vectors, first_norm_vectors, second_norm_vectors, grad_vectors, vector_rate
    )
    return (
        layer_out,
        input_grad,
        grad_qkv,
        second_qkv_new,
        weight_qkv_new,
        grad_out,
        second_out_new,
        weight_out_new,
        grad_gate_up,
        second_gu_new,
        weight_gu_new,
        grad_down,
        second_down_new,
        weight_down_new,
        grad_heads,
        second_heads_new,
        weight_heads_new,
        grad_vectors,
        second_vectors_new,
        weight_vectors_new,
    )


def solution(mesh):
    in_specs = (
        P("dp", None),
        P("dp", None),
        P("dp", None),
        P(None, "dp", "tensor"),
        P(None, "dp", "tensor"),
        P(None, "dp", "tensor"),
        P(("tensor", "dp"), None),
        P(("tensor", "dp"), None),
        P(("tensor", "dp"), None),
        P(None, "dp", "tensor"),
        P(None, "dp", "tensor"),
        P(None, "dp", "tensor"),
        P(("tensor", "dp"), None),
        P(("tensor", "dp"), None),
        P(("tensor", "dp"), None),
        P(None, ("tensor", "dp")),
        P(None, ("tensor", "dp")),
        P(None, ("tensor", "dp")),
        P(None, "dp"),
        P(None, "dp"),
        P(None, "dp"),
    )
    out_specs = (
        P("dp", None),
        P("dp", None),
        P(None, "dp", "tensor"),
        P(None, "dp", "tensor"),
        P(None, "dp", "tensor"),
        P(("tensor", "dp"), None),
        P(("tensor", "dp"), None),
        P(("tensor", "dp"), None),
        P(None, "dp", "tensor"),
        P(None, "dp", "tensor"),
        P(None, "dp", "tensor"),
        P(("tensor", "dp"), None),
        P(("tensor", "dp"), None),
        P(("tensor", "dp"), None),
        P(None, ("tensor", "dp")),
        P(None, ("tensor", "dp")),
        P(None, ("tensor", "dp")),
        P(None, "dp"),
        P(None, "dp"),
        P(None, "dp"),
    )
    return jax.shard_map(shards, mesh=mesh, in_specs=in_specs, out_specs=out_specs, check_vma=False)
```

time: 1560 us -> 356 us (0.23)
  waiting for transfers between devices: 823 us -> 0 us
  Pallas kernels: 0 us -> 325 us
  matrix products: 268 us -> 0 us
  blocking collectives: 164 us -> 0 us
  local copies, waits for them, and re-layouts: 137 us -> 11.8 us
  other arithmetic: 136 us -> 18.1 us
    unnamed x13 -> x0, waiting for transfers between devices: 523 us -> none
    pallas_call x0 -> x3, Pallas kernels: none -> 325 us  [the longest x1 122 us: back(): pl.pallas_call(functools.partial(back_kernel, seq=seq, pairs=pairs, route...]
    dot_general x40 -> x0, matrix products: 268 us -> none  [the longest x8 60.1 us: block_scores(): jnp.einsum('qhd,khd->hqk', q_rows, k_seq, preferred_element_type=jnp.floa...]
    reduce_scatter x2 -> x0, waiting for transfers between devices: 157 us -> none  [the longest x1 141 us: shards(): lax.psum_scatter(grad_down, 'dp', scatter_dimension=0, tiled=True)]
    all_gather x3 -> x0, blocking collectives: 122 us -> none  [the longest x1 42.2 us: shards(): lax.all_gather(weight_out.astype(jnp.bfloat16), 'dp', axis=0, tiled=True)]
    all_gather x3 -> x0, waiting for transfers between devices: 77.3 us -> none  [the longest x1 60.8 us: shards(): lax.all_gather(weight_gate_up.astype(jnp.bfloat16), 'dp', axis=1, tiled=T...]
    psum x4 -> x0, waiting for transfers between devices: 65.6 us -> none  [the longest x1 24.5 us: shards(): lax.psum(back_part.astype(jnp.bfloat16), 'tensor').astype(jnp.float32)]
    reduce_sum x15 -> x0, other arithmetic: 59.1 us -> none  [the longest x4 19.3 us: layer_norm(): centred = values - jnp.mean(values, axis=-1, keepdims=True)]
  transfers between devices with their start and end apart: 11 -> 0, of which waited for: 9 -> 0; matrix products, arithmetic and copies ran while one was open for 9% -> 0% of each run, Pallas kernels for 0% -> 0%
where the time goes in v2:
time: 356 us; the launch traced here: 355 us
  Pallas kernels  325 us (91%)
  other arithmetic  18.1 us (5%)
  local copies, waits for them, and re-layouts  11.8 us (3%)
    pallas_call x1, Pallas kernels, back(): pl.pallas_call(functools.partial(back_kernel, seq=seq, pairs=pairs, route...  122 us
    pallas_call x1, Pallas kernels, front(): pl.pallas_call(functools.partial(front_kernel, seq=seq, pairs=pairs, rout...  110 us
    pallas_call x1, Pallas kernels, middle(): pl.pallas_call(functools.partial(mid_kernel, tiles=tiles, ff=ff), out_sha...  92.9 us
    sub x6, other arithmetic, adam_update(): weight_old - step_rate * (first_hat / (jnp.sqrt(second_hat) + adam_epsilo...  10.3 us
    unnamed x26, local copies, waits for them, and re-layouts  7.26 us

profile of v2, /device:TPU:0, one launch (start us, length us, event | category | flops | bytes accessed | tf_op | source)
XLA Modules:
  0.0 355.4 jit_solution(9041584975538966226)
XLA Ops:
  0.7 0.0 copy-start.10
  0.7 1.2 dynamic-slice_multiply_fusion.refs_3_.refs_8_
  1.9 0.7 convert_element_type.25
  2.6 0.7 convert_element_type.24
  3.3 1.3 broadcast_in_dim.12.refs_2_.refs_7_
  4.6 0.2 dynamic_update_slice.6
  4.9 0.3 dynamic_update_slice.7.refs_5_
  5.2 0.0 copy-start.9
  5.2 0.9 convert_element_type.29
  6.1 0.6 pad.4.refs_9_
  6.7 1.6 convert_element_type.23
  8.3 1.6 convert_element_type.28.refs_8_
  9.9 1.1 convert.4
  11.0 0.7 slice_bitcast_fusion
  11.8 1.3 copy.42.refs_1_.refs_6_
  13.1 109.5 %front.1 = (bf16[2048,384]{1,0:T(8,128)(2,1)}, bf16[2048,384]{1,0:T(8,128)(2,1)}, bf16[2048,384]{1,0:T(8,128)(2,1)}, bf16[2048,384]{1,0:T(8,128)(2,1)}, f32[6,8,...) custom-call(bf16[2048,768]{1,0:T(8,128)(2,1)} %refs_9_.1, ...), custom_call_target="tpu_custom_call" | custom-call | tf_op jit(solution)/shard_map/front/pallas_call | solution.py:430
  122.7 92.9 %middle.1 = (bf16[2048,768]{1,0:T(8,128)(2,1)}, bf16[2048,768]{1,0:T(8,128)(2,1)}, bf16[2048,384]{1,0:T(8,128)(2,1)}, bf16[768,1536]{1,0:T(8,128)(2,1)}, bf16[76...) custom-call(bf16[2048,384]{1,0:T(8,128)(2,1)} %get-tuple-element.46.ctx_ref.ref, ...), custom_call_target="tpu_custom_call" | custom-call | tf_op jit(solution)/shard_map/middle/pallas_call | solution.py:585
  215.6 122.2 %back.1 = (bf16[2048,768]{1,0:T(8,128)(2,1)}, f32[48,1536]{1,0:T(8,128)}, f32[48,1536]{1,0:T(8,128)}, f32[96,768]{1,0:T(8,128)}, f32[32,768]{1,0:T(8,128)}, /*index=5*/f32[144,384]{1,0:T(8,128)}, f32[8,128]{1,0:T(8,128)}) custom-call(bf16[2048,384]{1,0:T(8,128)(2,1)} %get-tuple-element.53.refs_0_, bf16[2048,384]{1,0:T(8,128)(2,1)} %get-tuple-element.54.refs_1_, ...), custom_call_target="tpu_custom_call" | custom-call | tf_op jit(solution)/shard_map/back/pallas_call | solution.py:770
  337.7 0.0 copy-start.2
  337.8 0.0 copy-start.6
  337.8 1.5 multiply_subtract_fusion.5
  339.3 1.3 multiply_subtract_fusion.4
  340.6 1.7 multiply_subtract_fusion.3
  342.3 2.2 multiply_subtract_fusion.2
  344.5 2.3 multiply_subtract_fusion.1
  346.8 1.4 multiply_subtract_fusion
  348.1 1.1 copy-done
  349.3 1.7 copy.50
  350.9 1.4 copy-done.1
  352.3 1.7 copy.51
  354.0 0.7 copy.52
  354.7 0.7 copy.53
  (17 shorter events, 0.0 us)
Async XLA Ops:
  0.7 11.1 %copy-start.10 = (s32[2,1024]{1,0:T(2,128)S(1)}, s32[2,1024]{1,0:T(2,128)}, u32[]{:S(2)}) copy-start(s32[2,1024]{1,0:T(2,128)} %param.23) | copy-start | bytes 24580
  5.2 7.9 %copy-start.9 = (bf16[16,768]{1,0:T(8,128)(2,1)}, bf16[16,768]{1,0:T(8,128)(2,1)S(1)}, u32[]{:S(2)}) copy-start(bf16[16,768]{1,0:T(8,128)(2,1)S(1)} %dynamic_update_slice.7.refs_5_) | copy-start | bytes 73732
  337.7 9.0 %copy-start.2 = (f32[2,48,1536]{2,1,0:T(8,128)S(1)}, f32[2,48,1536]{2,1,0:T(8,128)}, u32[]{:S(2)}) copy-start(f32[2,48,1536]{2,1,0:T(8,128)} %param.31) | copy-start | bytes 1769476
  337.7 9.0 %copy-start.5 = (f32[2,48,1536]{2,1,0:T(8,128)S(1)}, f32[2,48,1536]{2,1,0:T(8,128)}, u32[]{:S(2)}) copy-start(f32[2,48,1536]{2,1,0:T(8,128)} %param.32) | copy-start | bytes 1769476
  337.8 9.0 %copy-start.6 = (f32[2,48,1536]{2,1,0:T(8,128)S(1)}, f32[2,48,1536]{2,1,0:T(8,128)}, u32[]{:S(2)}) copy-start(f32[2,48,1536]{2,1,0:T(8,128)} %param.33) | copy-start | bytes 1769476
  337.8 9.0 %copy-start.7 = (f32[48,1536]{1,0:T(8,128)S(1)}, f32[48,1536]{1,0:T(8,128)}, u32[]{:S(2)}) copy-start(f32[48,1536]{1,0:T(8,128)} %get-tuple-element.68) | copy-start | bytes 884740
  337.8 9.0 %copy-start.8 = (f32[48,1536]{1,0:T(8,128)S(1)}, f32[48,1536]{1,0:T(8,128)}, u32[]{:S(2)}) copy-start(f32[48,1536]{1,0:T(8,128)} %get-tuple-element.69) | copy-start | bytes 884740
  346.7 2.5 copy-start
  349.3 3.0 copy-start.1
  352.3 1.7 copy-start.4
  352.3 2.4 copy-start.3
